TPU v7x, 32 devices: a whole 2x2x4 slice. The times are simulated.
32 devices in a mesh: dp: 4 (over z), ctx: 8 (over y, x, core).
Axes of the slice: x: 2, y: 2, z: 4, core: 2. Of those that a mesh axis runs over, the one named last changes fastest.
Arguments:
- tokens: bfloat16 [8192, 2048], P(('dp', 'ctx')), parts along dimension 0, may hold values from -80 to 80
- qkv_weight: bfloat16 [2048, 3072], P('ctx'), may hold values from -0.125 to 0.125
- out_weight: bfloat16 [1024, 2048], P('ctx'), may hold values from -0.1875 to 0.1875
- prior_state: float32 [32, 128, 128], P('dp'), parts along dimension 0, may hold values from -240 to 240
- expert_ids: int32 [8192, 4], P(('dp', 'ctx')), parts along dimension 0, may hold values from 0 to 7, all different within a row; in each aligned block of 256 rows (0 to 255, 256 to 511, ...) at most 192 rows name the same one
- gate_weights: float32 [8192, 4], P(('dp', 'ctx')), parts along dimension 0, may hold values from 0.1 to 1
- expert_in: bfloat16 [8, 2048, 2048], P('ctx'), may hold values from -0.125 to 0.125
- expert_out: bfloat16 [8, 1024, 2048], P('ctx'), may hold values from -0.1875 to 0.1875
Outputs:
- layer_out: bfloat16 [8192, 2048], P(('dp', 'ctx')), parts along dimension 0
There are 4 independent parts, one for each index of `dp`. A program takes and returns all parts, laid end to end along the dimension named above; an argument that names none is the same for every part. Nothing has to cross between parts.
Inputs may be any that keep to these rules, and one draw needn't show every extreme that they name: `expert_ids`: within the 256 rows of one device no expert is named more than 192 times, and in some device's rows some expert is named exactly 192 times.
All inputs are finite; a program needn't handle non-finite values.
Results may differ from a plain program's by a relative error of at most 0.006.
Values may be sent and summed in bfloat16 or wider, within the bound.
A program may use at most 128 MiB of HBM per device.

v0:
```python
import jax
import jax.numpy as jnp
from jax import lax
from jax.sharding import PartitionSpec as P

HEADS = 8
HD = 128
FF = 1024


EPSILON = 1e-05


def prefix(x, axis, combine, identity):
    length, index = (lax.axis_size(axis), lax.axis_index(axis))
    everything = lax.all_gather(x.astype(jnp.bfloat16), axis)
    start = jnp.broadcast_to(jnp.asarray(identity, x.dtype), x.shape)

    def step(k, before):
        reached = k < index
        new = combine(before, everything[k].astype(x.dtype))
        return jnp.where(reached, new, before)

    return lax.fori_loop(0, length, step, start)


def rms_rows(matrix):
    return matrix * lax.rsqrt(jnp.mean(matrix * matrix, axis=-1, keepdims=True) + EPSILON)


def combine_add(earlier, later):
    return earlier + later


def shards(
    tokens, qkv_weight, out_weight, prior_state, expert_ids, gate_weights, expert_in, expert_out
):
    tok_rows = tokens.shape[0]
    model_width = tokens.shape[1]
    width_heads = HEADS * HD
    groups = lax.axis_size("ctx")
    local_experts = expert_in.shape[0]
    experts = local_experts * groups
    top_count = expert_ids.shape[1]
    capacity = 3 * tok_rows * top_count // (2 * experts)
    normed = rms_rows(tokens.astype(jnp.float32)).astype(jnp.bfloat16)
    columns = normed
    projected = jnp.dot(
        columns,
        lax.all_gather(qkv_weight, "ctx", axis=0, tiled=True),
        preferred_element_type=jnp.float32,
    )
    queries = (
        jax.nn.silu(projected[:, :width_heads]).astype(jnp.bfloat16).reshape(tok_rows, HEADS, HD)
    )
    key_rows = (
        jax.nn.silu(projected[:, width_heads : 2 * width_heads])
        .astype(jnp.bfloat16)
        .reshape(tok_rows, HEADS, HD)
    )
    value_rows = projected[:, 2 * width_heads :].astype(jnp.bfloat16).reshape(tok_rows, HEADS, HD)
    local_state = jnp.einsum(
        "thd,the->hde", key_rows, value_rows, preferred_element_type=jnp.float32
    )
    earlier_sum = prefix(local_state, "ctx", combine_add, jnp.zeros_like(local_state))
    carried = prior_state + earlier_sum
    scores = jnp.einsum("thd,shd->hts", queries, key_rows, preferred_element_type=jnp.float32)
    causal = (
        jnp.arange(tok_rows, dtype=jnp.int32)[:, None]
        >= jnp.arange(tok_rows, dtype=jnp.int32)[None, :]
    )
    scores = jnp.where(causal[None], scores, jnp.float32(0.0)).astype(jnp.bfloat16)
    inside = jnp.einsum("hts,she->the", scores, value_rows, preferred_element_type=jnp.float32)
    from_state = jnp.einsum(
        "thd,hde->the", queries.astype(jnp.float32), carried, precision=lax.Precision.HIGHEST
    )
    head_normed = rms_rows(from_state + inside).astype(jnp.bfloat16).reshape(tok_rows, width_heads)
    columns = head_normed
    attended = jnp.dot(
        columns,
        lax.all_gather(out_weight, "ctx", axis=0, tiled=True),
        preferred_element_type=jnp.float32,
    )
    hidden = (tokens.astype(jnp.float32) + attended).astype(jnp.bfloat16)
    moe_in = rms_rows(hidden.astype(jnp.float32)).astype(jnp.bfloat16)
    flat_ids = expert_ids.reshape(-1)
    onehot = (flat_ids[:, None] == jnp.arange(experts, dtype=jnp.int32)[None, :]).astype(jnp.int32)
    before = jnp.cumsum(onehot, axis=0) - onehot
    slot_index = jnp.sum(before * onehot, axis=1)
    places = flat_ids * capacity + slot_index
    repeated = jnp.repeat(moe_in, top_count, axis=0)
    outgoing = jnp.zeros((experts * capacity, model_width), jnp.bfloat16).at[places].set(repeated)
    outgoing = outgoing.reshape(experts, capacity, model_width)
    arrived = lax.all_to_all(outgoing, "ctx", split_axis=0, concat_axis=0, tiled=True)
    slot_count = arrived.shape[1]
    grouped = arrived.reshape(groups, local_experts, slot_count, model_width)
    gate_up = jnp.einsum("nxid,xdf->nxif", grouped, expert_in, preferred_element_type=jnp.float32)
    middle = (jax.nn.silu(gate_up[..., :FF]) * gate_up[..., FF:]).astype(jnp.bfloat16)
    result = jnp.einsum(
        "nxif,xfd->nxid", middle, expert_out, preferred_element_type=jnp.float32
    ).astype(jnp.bfloat16)
    finished = result.reshape(groups * local_experts, slot_count, model_width)
    returned = lax.all_to_all(finished, "ctx", split_axis=0, concat_axis=0, tiled=True).reshape(
        experts * capacity, model_width
    )
    picked = returned[places].reshape(tok_rows, top_count, model_width).astype(jnp.float32)
    combined = jnp.sum(gate_weights[:, :, None] * picked, axis=1)
    return (hidden.astype(jnp.float32) + combined).astype(jnp.bfloat16)


def solution(mesh):
    return jax.shard_map(
        shards,
        mesh=mesh,
        in_specs=(
            P(("dp", "ctx"), None),
            P("ctx", None),
            P("ctx", None),
            P("dp", None, None),
            P(("dp", "ctx"), None),
            P(("dp", "ctx"), None),
            P("ctx", None, None),
            P("ctx", None, None),
        ),
        out_specs=P(("dp", "ctx"), None),
        check_vma=False,
    )
```

profile of v0, /device:TPU:0, one launch (start us, length us, event | category | flops | bytes accessed | tf_op | source)
XLA Modules:
  0.0 401.1 jit_solution(15243015188607697220)
XLA Ops:
  6.5 0.0 all-gather.5.cloned.1.call-start
  6.5 0.7 all-gather.5.cloned.1.call-update
  7.3 0.0 all-gather.9.cloned.1.call-start
  7.3 1.5 fusion.12
  8.8 75.3 %all-gather.5.cloned.1.call-done = bf16[2048,3072]{1,0:T(8,128)(2,1)} async-done(((bf16[256,3072]{1,0:T(8,128)(2,1)}), bf16[2048,3072]{1,0:T(8,128)(2,1)}) %all-gather.5.cloned.1.call-update) | async-done | bytes 12582928 | tf_op jit(solution)/shard_map/all_gather | solution.py:50
  84.1 6.8 %fusion.20 = f32[256,3072]{1,0:T(8,128)S(1)} fusion(bf16[2048,3072]{1,0:T(8,128)(2,1)} %all-gather.5.cloned.1.call-done, bf16[256,2048]{1,0:T(8,128)(2,1)} %param.10, f32[256]{0:T(256)S(1)} %add_rsqrt_fusion.2), kind=kOutput, calls=%fused_computation.31 | convolution fusion | flops 3222798336 | bytes 16778240 | tf_op jit(solution)/shard_map/dot_general | solution.py:48
  90.9 0.0 copy-start.1
  90.9 0.6 fusion.34
  91.5 0.1 slice.55
  91.6 0.2 copy.36
  91.8 1.1 convolution_convert_fusion.1
  92.8 0.0 all-gather.9.cloned.1.call-update
  92.8 0.0 copy-start
  92.9 0.2 all-gather.7.cloned.1.call-start
  93.1 0.5 all-gather.7.cloned.1.call-update
  93.6 0.0 copy-done.1
  93.6 0.1 copy.33
  93.8 0.1 eq.29
  93.9 0.1 eq.25
  94.0 2.3 reduce-window.6
  96.3 0.3 slice_reduce_fusion
  96.6 0.2 reduce-window.9
  96.7 0.1 copy.32
  96.9 0.1 mul.85
  97.0 0.1 add_bitcast_fusion
  97.2 23.7 %all-gather.9.cloned.1.call-done = bf16[64,128,128]{2,1,0:T(8,128)(2,1)} async-done(((bf16[8,128,128]{2,1,0:T(8,128)(2,1)}), bf16[64,128,128]{2,1,0:T(8,128)(2,1)}) %all-gather.9.cloned.1.call-update) | async-done | bytes 2097168 | tf_op jit(solution)/shard_map/all_gather | solution.py:16
  120.9 10.1 %while.14 = (s32[]{:T(128)}, f32[8,128,128]{2,1,0:T(8,128)S(1)}, s32[]{:T(128)}, bf16[8,8,128,128]{3,2,1,0:T(8,128)(2,1)}, s32[]{:T(128)}, /*index=5*/s32[]{:T(128)}) while((s32[]{:T(128)}, f32[8,128,128]{2,1,0:T(8,128)S(1)}, s32[]{:T(128)}, bf16[8,8,128,128]{3,2,1,0:T(8,128)(2,1)}, s32[]{:T(128)}, /*index=5*/s32[]{:T(128)}) %tuple.44), condition=%wide.region_2.3_spmd.clone, body=%wide.region_1.2_spmd.clone.sunk | while | flops 524292 | bytes 1310813 | solution.py:24
  120.9 1.2 add_select_fusion.2
  122.1 1.2 add_select_fusion.2
  123.4 1.2 add_select_fusion.2
  124.7 1.2 add_select_fusion.2
  125.9 1.2 add_select_fusion.2
  127.2 1.2 add_select_fusion.2
  128.4 1.3 add_select_fusion.2
  129.7 1.3 add_select_fusion.2
  131.0 0.0 copy-done
  131.0 1.6 fusion.27
  132.6 2.0 multiply_reduce_fusion.1
  134.6 0.1 multiply_convert_fusion
  134.7 24.9 %all-gather.7.cloned.1.call-done = bf16[1024,2048]{1,0:T(8,128)(2,1)} async-done(((bf16[128,2048]{1,0:T(8,128)(2,1)}), bf16[1024,2048]{1,0:T(8,128)(2,1)}) %all-gather.7.cloned.1.call-update) | async-done | bytes 4194320 | tf_op jit(solution)/shard_map/all_gather | solution.py:81
  159.5 3.9 fusion.14
  163.4 0.2 fusion.15
  163.7 4.1 %broadcast_in_dim.35 = bf16[256,4,2048]{2,1,0:T(4,128)(2,1)} broadcast(bf16[256,2048]{1,0:T(8,128)(2,1)S(1)} %fusion.15), dimensions={0,2} | broadcast | bytes 5242880 | tf_op jit(solution)/shard_map/broadcast_in_dim | solution.py:91
  167.8 6.9 %reshape.150 = bf16[1024,2048]{1,0:T(8,128)(2,1)} reshape(bf16[256,4,2048]{2,1,0:T(4,128)(2,1)} %broadcast_in_dim.35) | data formatting | bytes 8388608 | tf_op jit(solution)/shard_map/reshape | solution.py:91
  174.7 11.2 %scatter_custom_fusion = bf16[1536,2048]{1,0:T(8,128)(2,1)} fusion(s32[1024]{0:T(1024)S(1)} %bitcast.84, bf16[1024,2048]{1,0:T(8,128)(2,1)} %reshape.150, bf16[]{:T(256)} %constant.55.clone.1), kind=kCustom, calls=%fused_computation.12 | custom fusion | bytes 6291968 | tf_op jit(solution)/shard_map/scatter | solution.py:92
  185.9 75.2 %all_to_all.10 = bf16[8,192,2048]{2,1,0:T(8,128)(2,1)S(1)} all-to-all(bf16[8,192,2048]{2,1,0:T(8,128)(2,1)} %bitcast.78), channel_id=1, replica_groups=mesh['dp'=4,'ctx'=8] {'ctx'}, dimensions={0} | all-to-all | bytes 12582912 | tf_op jit(solution)/shard_map/all_to_all | solution.py:94
  261.2 0.0 copy-start.3
  261.2 16.2 %fusion.3 = f32[8,1,192,2048]{3,2,0,1:T(8,128)S(1)} fusion(bf16[8,192,2048]{2,1,0:T(8,128)(2,1)S(1)} %all_to_all.10, bf16[1,2048,2048]{2,1,0:T(8,128)(2,1)} %param.16), kind=kOutput, calls=%fused_computation.8 | convolution fusion | flops 12884901888 | bytes 27262976 | tf_op jit(solution)/shard_map/nxid,xdf->nxif/dot_general | solution.py:97
  277.4 0.0 copy-done.3
  277.4 8.7 %convolution_convert_fusion = bf16[8,192,2048]{2,1,0:T(8,128)(2,1)} fusion(bf16[1,1024,2048]{2,1,0:T(8,128)(2,1)S(1)} %copy-done.3, f32[8,1,192,2048]{3,2,0,1:T(8,128)S(1)} %fusion.3), kind=kOutput, calls=%fused_computation.9 | convolution fusion | flops 6455033856 | bytes 23068672 | tf_op jit(solution)/shard_map/nxif,xfd->nxid/dot_general | solution.py:99
  286.1 0.0 copy-start.2
  286.1 5.1 %all-to-all-start.1 = ((bf16[8,192,2048]{2,1,0:T(8,128)(2,1)}), bf16[8,192,2048]{2,1,0:T(8,128)(2,1)}, u32[]{:S(2)}, u32[]{:S(2)}) async-start(bf16[8,192,2048]{2,1,0:T(8,128)(2,1)} %convolution_convert_fusion), calls=%async_computation.1 | async-start | bytes 12582912 | tf_op jit(solution)/shard_map/all_to_all | solution.py:103
  291.2 0.0 copy-done.2
  291.2 0.1 copy.31
  291.4 71.2 %all-to-all-done.1 = bf16[8,192,2048]{2,1,0:T(8,128)(2,1)} async-done(((bf16[8,192,2048]{2,1,0:T(8,128)(2,1)}), bf16[8,192,2048]{2,1,0:T(8,128)(2,1)}, u32[]{:S(2)}, u32[]{:S(2)}) %all-to-all-start.1) | async-done | bytes 6291488 | tf_op jit(solution)/shard_map/all_to_all | solution.py:103
  362.5 12.4 %gather_fusion = bf16[1024,2048]{1,0:T(8,128)(2,1)} fusion(bf16[1536,2048]{1,0:T(8,128)(2,1)} %bitcast.17, s32[1024]{0:T(1024)S(1)} %broadcast_clamp_fusion), kind=kCustom, calls=%fused_computation | custom fusion | bytes 8392704 | tf_op jit(solution)/shard_map/gather | solution.py:106
  375.0 8.3 %reshape.137 = f32[256,4,2048]{2,1,0:T(4,128)} reshape(bf16[1024,2048]{1,0:T(8,128)(2,1)} %gather_fusion) | data formatting | bytes 12582912 | tf_op jit(solution)/shard_map/convert_element_type | solution.py:106
  383.3 10.0 %multiply_reduce_fusion = f32[256,2048]{1,0:T(8,128)S(1)} fusion(f32[256,4,2048]{2,1,0:T(4,128)} %reshape.137, f32[256,4]{1,0:T(8,128)S(1)} %copy.31), kind=kLoop, calls=%fused_computation.5 | loop fusion | flops 3670016 | bytes 10489856 | tf_op jit(solution)/shard_map/reduce_sum | solution.py:107
  393.3 1.3 fusion.16
  (10 shorter events, 0.1 us)
Async XLA Ops:
  6.5 77.6 %all-gather.5.cloned.1.call-start = ((), (), s32[]{:S(2)}) async-start(), calls=%async_computation.2 | async-start | bytes 14155776 | tf_op jit(solution)/shard_map/all_gather | solution.py:50
  7.3 113.6 %all-gather.9.cloned.1.call-start = ((), (), s32[]{:S(2)}) async-start(), calls=%async_computation.4 | async-start | bytes 2359296 | tf_op jit(solution)/shard_map/all_gather | solution.py:16
  90.9 2.7 copy-start.1
  92.8 38.1 %copy-start = (f32[8,128,128]{2,1,0:T(8,128)S(1)}, f32[8,128,128]{2,1,0:T(8,128)}, u32[]{:S(2)}) copy-start(f32[8,128,128]{2,1,0:T(8,128)} %param.13) | copy-start | bytes 1572868
  92.9 66.7 %all-gather.7.cloned.1.call-start = ((), (), s32[]{:S(2)}) async-start(), calls=%async_computation.3 | async-start | bytes 4718592 | tf_op jit(solution)/shard_map/all_gather | solution.py:81
  261.2 16.2 %copy-start.3 = (bf16[1,1024,2048]{2,1,0:T(8,128)(2,1)S(1)}, bf16[1,1024,2048]{2,1,0:T(8,128)(2,1)}, u32[]{:S(2)}) copy-start(bf16[1,1024,2048]{2,1,0:T(8,128)(2,1)} %param.17) | copy-start | bytes 12582916
  286.1 5.1 %copy-start.2 = (f32[256,4]{0,1:T(4,128)S(1)}, f32[256,4]{0,1:T(4,128)}, u32[]{:S(2)}) copy-start(f32[256,4]{0,1:T(4,128)} %param.15) | copy-start | bytes 12292
  286.1 76.5 %all-to-all-start.1 = ((bf16[8,192,2048]{2,1,0:T(8,128)(2,1)}), bf16[8,192,2048]{2,1,0:T(8,128)(2,1)}, u32[]{:S(2)}, u32[]{:S(2)}) async-start(bf16[8,192,2048]{2,1,0:T(8,128)(2,1)} %convolution_convert_fusion), calls=%async_computation.1 | async-start | bytes 12582912 | tf_op jit(solution)/shard_map/all_to_all | solution.py:103
Sparse Core Ops, SparseCore 0:
  9.2 74.8 all-gather.4
  93.0 27.8 all-gather.8
  122.8 36.7 all-gather.6
where the time goes:
time: 402 us; the launch traced here: 401 us
  waiting for transfers between devices  196 us (49%)
  blocking collectives  75.2 us (19%)
  local copies, waits for them, and re-layouts  44.3 us (11%)
  matrix products  40.2 us (10%)
  other arithmetic  26.2 us (7%)
  between operations  13.3 us (3%)
  starting transfers between devices  5.39 us (1%)
    all_gather x1, waiting for transfers between devices, shards(): lax.all_gather(qkv_weight, 'ctx', axis=0, tiled=True)  75.3 us
    all_to_all x1, blocking collectives, shards(): lax.all_to_all(outgoing, 'ctx', split_axis=0, concat_axis=0, tiled=True)  75.2 us
    all_to_all x1, waiting for transfers between devices, shards(): lax.all_to_all(finished, 'ctx', split_axis=0, concat_axis=0, tiled=True)  71.2 us
    all_gather x1, waiting for transfers between devices, shards(): lax.all_gather(out_weight, 'ctx', axis=0, tiled=True)  24.9 us
    all_gather x1, waiting for transfers between devices, prefix(): everything = lax.all_gather(x.astype(jnp.bfloat16), axis)  23.7 us
    dot_general x1, matrix products, shards(): jnp.einsum('nxid,xdf->nxif', grouped, expert_in, preferred_element_type=j...  16.2 us
    gather x1, local copies, waits for them, and re-layouts, shards(): returned[places].reshape(tok_rows, top_count, model_width)  12.4 us
    scatter x1, local copies, waits for them, and re-layouts, shards(): jnp.zeros((experts * capacity, model_width), jnp.bfloat16).at[places]  11.2 us
  transfers between devices with their start and end apart: 4, of which 4 were waited for; matrix products, arithmetic and copies ran while one was open for 5% of the time, Pallas kernels for 0%

commit v1 on v0

--- a/solution.py
+++ b/solution.py
@@ -1,6 +1,8 @@
 import jax
 import jax.numpy as jnp
 from jax import lax
+from jax.experimental import pallas as pl
+from jax.experimental.pallas import tpu as pltpu
 from jax.sharding import PartitionSpec as P
 
 HEADS = 8
@@ -11,25 +13,258 @@
 EPSILON = 1e-05
 
 
-def prefix(x, axis, combine, identity):
+def prefix(x, axis):
     length, index = (lax.axis_size(axis), lax.axis_index(axis))
     everything = lax.all_gather(x.astype(jnp.bfloat16), axis)
-    start = jnp.broadcast_to(jnp.asarray(identity, x.dtype), x.shape)
-
-    def step(k, before):
-        reached = k < index
-        new = combine(before, everything[k].astype(x.dtype))
-        return jnp.where(reached, new, before)
-
-    return lax.fori_loop(0, length, step, start)
+    reached = jnp.arange(length) < index
+    reached = reached.reshape((length,) + (1,) * x.ndim)
+    return jnp.sum(jnp.where(reached, everything.astype(x.dtype), 0.0), axis=0)
 
 
 def rms_rows(matrix):
     return matrix * lax.rsqrt(jnp.mean(matrix * matrix, axis=-1, keepdims=True) + EPSILON)
 
 
-def combine_add(earlier, later):
-    return earlier + later
+CHIPS = 4
+TILE = 256
+MESH = pl.DeviceIdType.MESH
+
+
+def moe_kernel(
+    hidden_ref, gates_ref, win_hbm, wout_hbm, out_ref,
+    xg, win, wout, gath, part, pair, sendb, final, mid,
+    send_sem, recv_sem, gsend, grecv, wsem,
+):
+    me = lax.axis_index("ctx")
+    core = me % 2
+    chip_x = (me // 2) % 2
+    chip_y = me // 4
+    rows = hidden_ref.shape[0]
+    half = rows // 2
+    width = hidden_ref.shape[1]
+    ff = mid.shape[1]
+
+    def peer(relation, same_core=True):
+        x = 1 - chip_x if relation % 2 else chip_x
+        y = 1 - chip_y if relation // 2 else chip_y
+        return (y * 2 + x) * 2 + (core if same_core else 1 - core)
+
+    barrier = pltpu.get_barrier_semaphore()
+    for k in range(1, 8):
+        pl.semaphore_signal(
+            barrier, inc=1, device_id={"ctx": (me + k) % 8}, device_id_type=MESH
+        )
+    load_in = pltpu.make_async_copy(win_hbm.at[0], win, wsem.at[0])
+    load_out = pltpu.make_async_copy(wout_hbm.at[0], wout, wsem.at[1])
+    load_in.start()
+    load_out.start()
+
+    for h in range(2):
+        block = hidden_ref[pl.ds(h * half, half), :].astype(jnp.float32)
+        scale = lax.rsqrt(jnp.mean(block * block, axis=-1, keepdims=True) + EPSILON)
+        xg[0, h, core] = (block * scale).astype(jnp.bfloat16)
+    pl.semaphore_wait(barrier, 7)
+
+    copies = {}
+
+    def send(name, source, target, device):
+        index = len(copies)
+        copies[name] = pltpu.make_async_remote_copy(
+            src_ref=source,
+            dst_ref=target,
+            send_sem=send_sem.at[index],
+            recv_sem=recv_sem.at[index],
+            device_id={"ctx": device},
+            device_id_type=MESH,
+        )
+        copies[name].start()
+
+    def own(relation, h):
+        send(("link", relation, h), xg.at[0, h, core], xg.at[relation, h, core], peer(relation))
+
+    def across(relation, h):
+        slot = xg.at[relation, h, core]
+        send(("core", relation, h), slot, slot, peer(0, False))
+
+    def arrived(kind, relation, h):
+        copies[(kind, relation, h)].wait_recv()
+
+    own(1, 0)
+    own(2, 1)
+    across(0, 0)
+    across(0, 1)
+    own(1, 1)
+    own(2, 0)
+    gath[me] = gates_ref[...]
+    gate_copies = []
+    for k in range(1, 8):
+        gate_copies.append(
+            pltpu.make_async_remote_copy(
+                src_ref=gates_ref,
+                dst_ref=gath.at[me],
+                send_sem=gsend.at[k - 1],
+                recv_sem=grecv.at[k - 1],
+                device_id={"ctx": (me + k) % 8},
+                device_id_type=MESH,
+            )
+        )
+        gate_copies[-1].start()
+    load_in.wait()
+    load_out.wait()
+    for copy in gate_copies:
+        copy.wait_recv()
+
+    def expert(relation, halves):
+        count = len(halves) * rows
+        first = halves[0]
+
+        def operand():
+            if len(halves) == 2:
+                return xg[relation].reshape(count, width)
+            return xg[relation, first].reshape(count, width)
+
+        owner = (peer(relation) // 2) * 2
+        columns = []
+        for h in halves:
+            for c in range(2):
+                table = jnp.transpose(gath[owner + c, :, pl.ds(h * half, half)])
+                lane = lax.broadcasted_iota(jnp.int32, table.shape, 1)
+                columns.append(
+                    jnp.sum(jnp.where(lane == me, table, 0.0), axis=1, keepdims=True)
+                )
+
+        @pl.loop(0, ff // TILE)
+        def _(f):
+            at = pl.multiple_of(f * TILE, TILE)
+            rows_in = operand()
+            gate = jnp.dot(rows_in, win[:, pl.ds(at, TILE)], preferred_element_type=jnp.float32)
+            up = jnp.dot(
+                rows_in, win[:, pl.ds(ff + at, TILE)], preferred_element_type=jnp.float32
+            )
+            mid[pl.ds(0, count), pl.ds(at, TILE)] = (
+                gate / (1.0 + jnp.exp(-gate)) * up
+            ).astype(jnp.bfloat16)
+
+        @pl.loop(0, width // TILE)
+        def _(n):
+            at = pl.multiple_of(n * TILE, TILE)
+            result = jnp.dot(
+                mid[pl.ds(0, count), :],
+                wout[:, pl.ds(at, TILE)],
+                preferred_element_type=jnp.float32,
+            )
+            k = 0
+            for h in halves:
+                for c in range(2):
+                    part[relation, h, c, :, pl.ds(at, TILE)] = (
+                        result[k * half : (k + 1) * half] * columns[k]
+                    ).astype(jnp.bfloat16)
+                    k += 1
+
+        for h in halves:
+            send(("pair", relation, h), part.at[relation, h, 1 - core], pair.at[relation, h],
+                 peer(0, False))
+
+    def give(relation, halves):
+        for h in halves:
+            arrived("pair", relation, h)
+            sendb[relation - 1, h] = (
+                part[relation, h, core].astype(jnp.float32)
+                + pair[relation, h].astype(jnp.float32)
+            ).astype(jnp.bfloat16)
+            send(("sum", relation, h), sendb.at[relation - 1, h], final.at[relation - 1, h],
+                 peer(relation))
+
+    arrived("core", 0, 0)
+    arrived("core", 0, 1)
+    expert(0, (0, 1))
+    arrived("link", 1, 0)
+    send(("link", 3, 0), xg.at[1, 0, core], xg.at[3, 0, core], peer(2))
+    across(1, 0)
+    arrived("link", 2, 1)
+    send(("link", 3, 1), xg.at[2, 1, core], xg.at[3, 1, core], peer(1))
+    across(2, 1)
+    arrived("core", 1, 0)
+    expert(1, (0,))
+    arrived("core", 2, 1)
+    expert(2, (1,))
+    give(1, (0,))
+    arrived("link", 1, 1)
+    across(1, 1)
+    arrived("link", 2, 0)
+    across(2, 0)
+    give(2, (1,))
+    arrived("core", 1, 1)
+    expert(1, (1,))
+    arrived("core", 2, 0)
+    expert(2, (0,))
+    give(1, (1,))
+    arrived("link", 3, 0)
+    across(3, 0)
+    arrived("link", 3, 1)
+    across(3, 1)
+    give(2, (0,))
+    arrived("core", 3, 0)
+    expert(3, (0,))
+    arrived("core", 3, 1)
+    expert(3, (1,))
+    give(3, (0,))
+    give(3, (1,))
+    for h in range(2):
+        arrived("pair", 0, h)
+        span = pl.ds(h * half, half)
+        total = (
+            hidden_ref[span, :].astype(jnp.float32)
+            + part[0, h, core].astype(jnp.float32)
+            + pair[0, h].astype(jnp.float32)
+        )
+        for relation in range(1, CHIPS):
+            arrived("sum", relation, h)
+            total += final[relation - 1, h].astype(jnp.float32)
+        out_ref[span, :] = total.astype(jnp.bfloat16)
+    for copy in gate_copies:
+        copy.wait_send()
+    for copy in copies.values():
+        copy.wait_send()
+
+
+def moe_fused(hidden, gates, expert_in, expert_out):
+    rows, width = hidden.shape
+    ff = expert_out.shape[1]
+    half = rows // 2
+    bf16 = jnp.bfloat16
+    vmem = pl.BlockSpec(memory_space=pltpu.VMEM)
+    hbm = pl.BlockSpec(memory_space=pl.ANY)
+    copies = 34
+    return pl.pallas_call(
+        moe_kernel,
+        out_shape=jax.ShapeDtypeStruct((rows, width), bf16),
+        in_specs=[vmem, vmem, hbm, hbm],
+        out_specs=vmem,
+        scratch_shapes=[
+            pltpu.VMEM((CHIPS, 2, 2, half, width), bf16),
+            pltpu.VMEM(expert_in.shape[1:], bf16),
+            pltpu.VMEM(expert_out.shape[1:], bf16),
+            pltpu.VMEM((8,) + gates.shape, jnp.float32),
+            pltpu.VMEM((CHIPS, 2, 2, half, width), bf16),
+            pltpu.VMEM((CHIPS, 2, half, width), bf16),
+            pltpu.VMEM((CHIPS - 1, 2, half, width), bf16),
+            pltpu.VMEM((CHIPS - 1, 2, half, width), bf16),
+            pltpu.VMEM((2 * rows, ff), bf16),
+            pltpu.SemaphoreType.DMA((copies,)),
+            pltpu.SemaphoreType.DMA((copies,)),
+            pltpu.SemaphoreType.DMA((7,)),
+            pltpu.SemaphoreType.DMA((7,)),
+            pltpu.SemaphoreType.DMA((2,)),
+        ],
+        compiler_params=pltpu.CompilerParams(
+            collective_id=1, has_side_effects=True, vmem_limit_bytes=58 * 1024 * 1024
+        ),
+        cost_estimate=pl.CostEstimate(
+            flops=6 * 8 * rows * width * ff, bytes_accessed=6 * width * ff, transcendentals=0
+        ),
+        name="moe",
+    )(hidden, gates, expert_in, expert_out)
 
 
 def shards(
@@ -62,7 +297,7 @@
     local_state = jnp.einsum(
         "thd,the->hde", key_rows, value_rows, preferred_element_type=jnp.float32
     )
-    earlier_sum = prefix(local_state, "ctx", combine_add, jnp.zeros_like(local_state))
+    earlier_sum = prefix(local_state, "ctx")
     carried = prior_state + earlier_sum
     scores = jnp.einsum("thd,shd->hts", queries, key_rows, preferred_element_type=jnp.float32)
     causal = (
@@ -82,6 +317,10 @@
         preferred_element_type=jnp.float32,
     )
     hidden = (tokens.astype(jnp.float32) + attended).astype(jnp.bfloat16)
+    if groups == 8 and local_experts == 1:
+        named = expert_ids[None] == jnp.arange(experts, dtype=jnp.int32)[:, None, None]
+        gates = jnp.sum(jnp.where(named, gate_weights[None], 0.0), axis=2)
+        return moe_fused(hidden, gates, expert_in, expert_out)
     moe_in = rms_rows(hidden.astype(jnp.float32)).astype(jnp.bfloat16)
     flat_ids = expert_ids.reshape(-1)
     onehot = (flat_ids[:, None] == jnp.arange(experts, dtype=jnp.int32)[None, :]).astype(jnp.int32)

time: 402 us -> 280 us (0.70)
  Pallas kernels: 0 us -> 107 us
  blocking collectives: 75.2 us -> 0 us
  waiting for transfers between devices: 196 us -> 134 us
  local copies, waits for them, and re-layouts: 44.3 us -> 2.6 us
  matrix products: 40.2 us -> 16.8 us
  other arithmetic: 26.2 us -> 6.16 us
  starting transfers between devices: 5.39 us -> 0.08 us
    pallas_call x0 -> x1, Pallas kernels: none -> 107 us  [moe_fused(): pl.pallas_call(moe_kernel, out_shape=jax.ShapeDtypeStruct((rows, width),...]
    all_to_all x1 -> x0, blocking collectives: 75.2 us -> none  [shards(): lax.all_to_all(outgoing, 'ctx', split_axis=0, concat_axis=0, tiled=True)]
    all_to_all x1 -> x0, waiting for transfers between devices: 71.2 us -> none  [shards(): lax.all_to_all(finished, 'ctx', split_axis=0, concat_axis=0, tiled=True)]
    dot_general x2 -> x0, matrix products: 24.9 us -> none  [the longest x1 16.2 us: shards(): jnp.einsum('nxid,xdf->nxif', grouped, expert_in, preferred_element_type=j...]
    gather x1 -> x0, local copies, waits for them, and re-layouts: 12.4 us -> none  [shards(): returned[places].reshape(tok_rows, top_count, model_width)]
    scatter x1 -> x0, local copies, waits for them, and re-layouts: 11.2 us -> none  [shards(): jnp.zeros((experts * capacity, model_width), jnp.bfloat16).at[places]]
    select_n x9 -> x0, other arithmetic: 9.92 us -> none  [the longest x8 9.91 us: step(): return jnp.where(reached, new, before)]
    convert_element_type x1 -> x0, local copies, waits for them, and re-layouts: 8.31 us -> none  [shards(): returned[places].reshape(tok_rows, top_count, model_width)]
  transfers between devices with their start and end apart: 4 -> 3, of which waited for: 4 -> 3; matrix products, arithmetic and copies ran while one was open for 5% -> 4% of each run, Pallas kernels for 0% -> 0%
where the time goes in v1:
time: 280 us
  waiting for transfers between devices  134 us (48%)
  Pallas kernels  107 us (38%)
  matrix products  16.8 us (6%)
  between operations  13.2 us (5%)
  other arithmetic  6.16 us (2%)
    pallas_call x1, Pallas kernels, moe_fused(): pl.pallas_call(moe_kernel, out_shape=jax.ShapeDtypeStruct((rows, width),...  107 us
    all_gather x1, waiting for transfers between devices, shards(): lax.all_gather(qkv_weight, 'ctx', axis=0, tiled=True)  75.3 us
    all_gather x1, waiting for transfers between devices, shards(): lax.all_gather(out_weight, 'ctx', axis=0, tiled=True)  30.6 us
    all_gather x1, waiting for transfers between devices, prefix(): everything = lax.all_gather(x.astype(jnp.bfloat16), axis)  26.6 us
    dot_general x1, matrix products, shards(): jnp.dot(columns, lax.all_gather(qkv_weight, 'ctx', axis=0, tiled=True), p...  6.75 us
  transfers between devices with their start and end apart: 3, of which 3 were waited for; matrix products, arithmetic and copies ran while one was open for 4% of the time, Pallas kernels for 0%

profile of v1, /device:TPU:0, one launch (start us, length us, event | category | flops | bytes accessed | tf_op | source)
XLA Modules:
  0.0 279.7 jit_solution(8327572679118718617)
XLA Ops:
  6.5 0.0 all-gather.5.cloned.1.call-start
  6.5 0.7 all-gather.5.cloned.1.call-update
  7.3 0.0 all-gather.9.cloned.1.call-start
  7.3 1.5 fusion.2
  8.8 75.3 %all-gather.5.cloned.1.call-done = bf16[2048,3072]{1,0:T(8,128)(2,1)} async-done(((bf16[256,3072]{1,0:T(8,128)(2,1)}), bf16[2048,3072]{1,0:T(8,128)(2,1)}) %all-gather.5.cloned.1.call-update) | async-done | bytes 12582928 | tf_op jit(solution)/shard_map/all_gather | solution.py:285
  84.1 6.8 %fusion.7 = f32[256,3072]{1,0:T(8,128)S(1)} fusion(bf16[2048,3072]{1,0:T(8,128)(2,1)} %all-gather.5.cloned.1.call-done, bf16[256,2048]{1,0:T(8,128)(2,1)} %param.8, f32[256]{0:T(256)S(1)} %add_rsqrt_fusion.1), kind=kOutput, calls=%fused_computation.13 | convolution fusion | flops 3222798336 | bytes 16778240 | tf_op jit(solution)/shard_map/dot_general | solution.py:283
  90.9 0.0 copy-start.2
  90.9 0.0 copy-start.3
  90.9 0.6 fusion.21
  91.5 0.1 slice.23
  91.5 0.0 copy-start.1
  91.5 0.2 copy.31
  91.8 1.1 convolution_convert_fusion
  92.8 0.0 all-gather.9.cloned.1.call-update
  92.8 0.0 all-gather.7.cloned.1.call-start
  92.9 0.7 all-gather.7.cloned.1.call-update
  93.6 0.0 copy-done.2
  93.6 0.0 copy-done.3
  93.6 0.6 select_reduce_fusion.gates_ref
  94.2 26.6 %all-gather.9.cloned.1.call-done = bf16[64,128,128]{2,1,0:T(8,128)(2,1)} async-done(((bf16[8,128,128]{2,1,0:T(8,128)(2,1)}), bf16[64,128,128]{2,1,0:T(8,128)(2,1)}) %all-gather.9.cloned.1.call-update) | async-done | bytes 2097168 | tf_op jit(solution)/shard_map/all_gather | solution.py:18
  120.9 2.1 fusion
  123.0 0.0 copy-done.1
  123.0 1.6 fusion.14
  124.6 0.0 copy-start
  124.6 3.0 %multiply_reduce_fusion = (f32[256,8]{0,1:T(8,128)S(1)}, f32[256,8,128]{0,2,1:T(8,128)}) fusion(f32[8,128,256]{2,1,0:T(8,128)} %fusion.14, bf16[256,8,128]{0,2,1:T(8,128)(2,1)S(1)} %bitcast.33, pred[256,256]{1,0:T(8,128)(4,1)S(1)} %iota_compare_fusion, bf16[32,8,8,128]{3,2,1,0:T(8,128)(2,1)S(1)} %get-tuple-element.5, ...), kind=kOutput, calls=%fused_computation.16 | convolution fusion | flops 270268416 | bytes 3743744 | tf_op jit(solution)/shard_map/hts,she->the/dot_general | solution.py:308
  127.7 1.3 multiply_convert_fusion
  129.0 30.6 %all-gather.7.cloned.1.call-done = bf16[1024,2048]{1,0:T(8,128)(2,1)} async-done(((bf16[128,2048]{1,0:T(8,128)(2,1)}), bf16[1024,2048]{1,0:T(8,128)(2,1)}) %all-gather.7.cloned.1.call-update) | async-done | bytes 4194320 | tf_op jit(solution)/shard_map/all_gather | solution.py:316
  159.5 0.0 copy-done
  159.5 4.4 %fusion.1.hidden_ref = bf16[256,2048]{1,0:T(8,128)(2,1)} fusion(bf16[256,1024]{0,1:T(8,128)(2,1)S(1)} %bitcast.34, bf16[1024,2048]{1,0:T(8,128)(2,1)} %all-gather.7.cloned.1.call-done, bf16[256,2048]{1,0:T(8,128)(2,1)S(1)} %copy-done), kind=kOutput, calls=%fused_computation.5 | convolution fusion | flops 1075314688 | bytes 6815744 | tf_op jit(solution)/shard_map/dot_general | solution.py:314
  164.0 106.9 %moe.1 = bf16[256,2048]{1,0:T(8,128)(2,1)} custom-call(bf16[256,2048]{1,0:T(8,128)(2,1)} %fusion.1.hidden_ref, f32[8,256]{1,0:T(8,128)} %select_reduce_fusion.gates_ref, bf16[1,2048,2048]{2,1,0:T(8,128)(2,1)} %win_hbm.1, bf16[1,1024,2048]{2,1,0:T(8,128)(2,1)} %wout_hbm.1), custom_call_target="tpu_custom_call" | custom-call | flops 25769803776 | bytes 12582912 | tf_op jit(solution)/shard_map/moe/pallas_call | solution.py:239
  270.9 2.3 copy.57
  (4 shorter events, 0.0 us)
Async XLA Ops:
  6.5 77.6 %all-gather.5.cloned.1.call-start = ((), (), s32[]{:S(2)}) async-start(), calls=%async_computation | async-start | bytes 14155776 | tf_op jit(solution)/shard_map/all_gather | solution.py:285
  7.3 113.6 %all-gather.9.cloned.1.call-start = ((), (), s32[]{:S(2)}) async-start(), calls=%async_computation.2 | async-start | bytes 2359296 | tf_op jit(solution)/shard_map/all_gather | solution.py:18
  90.9 2.7 copy-start.2
  90.9 2.7 copy-start.3
  91.5 31.5 %copy-start.1 = (f32[8,128,128]{2,1,0:T(8,128)S(1)}, f32[8,128,128]{2,1,0:T(8,128)}, u32[]{:S(2)}) copy-start(f32[8,128,128]{2,1,0:T(8,128)} %param.11) | copy-start | bytes 1572868
  92.8 66.7 %all-gather.7.cloned.1.call-start = ((), (), s32[]{:S(2)}) async-start(), calls=%async_computation.1 | async-start | bytes 4718592 | tf_op jit(solution)/shard_map/all_gather | solution.py:316
  124.6 34.9 %copy-start = (bf16[256,2048]{1,0:T(8,128)(2,1)S(1)}, bf16[256,2048]{1,0:T(8,128)(2,1)}, u32[]{:S(2)}) copy-start(bf16[256,2048]{1,0:T(8,128)(2,1)} %param.8) | copy-start | bytes 3145732
Sparse Core Ops, SparseCore 0:
  9.2 74.8 all-gather.4
  93.0 27.8 all-gather.8
  122.8 36.7 all-gather.6

commit v2 on v1

--- a/solution.py
+++ b/solution.py
@@ -267,6 +267,248 @@
     )(hidden, gates, expert_in, expert_out)
 
 
+def attention_kernel(
+    tokens_ref, wsplit_ref, ow_ref, prior_ref, hidden_ref,
+    tk, wbuf, acc, qkvb, sbuf, tsend, trecv, mixed, hnbuf, hall, outw,
+    send_sem, recv_sem,
+):
+    me = lax.axis_index("ctx")
+    core = me % 2
+    chip_x = (me // 2) % 2
+    chip_y = me // 4
+    rows, width = tokens_ref.shape
+    half = rows // 2
+    group = chip_x * 2 + core
+    wide = 2 * HD
+    depth = wbuf.shape[1]
+
+    def peer(relation, same_core=True):
+        x = 1 - chip_x if relation % 2 else chip_x
+        y = 1 - chip_y if relation // 2 else chip_y
+        return (y * 2 + x) * 2 + (core if same_core else 1 - core)
+
+    barrier = pltpu.get_barrier_semaphore()
+    for k in range(1, 8):
+        pl.semaphore_signal(
+            barrier, inc=1, device_id={"ctx": (me + k) % 8}, device_id_type=MESH
+        )
+    pl.semaphore_wait(barrier, 7)
+
+    copies = {}
+
+    def send(name, source, target, device):
+        index = len(copies)
+        copies[name] = pltpu.make_async_remote_copy(
+            src_ref=source,
+            dst_ref=target,
+            send_sem=send_sem.at[index],
+            recv_sem=recv_sem.at[index],
+            device_id={"ctx": device},
+            device_id_type=MESH,
+        )
+        copies[name].start()
+
+    def arrived(*name):
+        copies[name].wait_recv()
+
+    for same in (True, False):
+        other = core if same else 1 - core
+        send(("w", 1, same), wsplit_ref.at[(1 - chip_x) * 2 + other], wbuf.at[me], peer(1, same))
+        send(("w", 2, same), wsplit_ref.at[chip_x * 2 + other], wbuf.at[me], peer(2, same))
+    send(("w", 0), wsplit_ref.at[chip_x * 2 + 1 - core], wbuf.at[me], peer(0, False))
+    wbuf[me] = wsplit_ref[group]
+    for h in range(2):
+        block = tokens_ref[pl.ds(h * half, half), :].astype(jnp.float32)
+        scale = lax.rsqrt(jnp.mean(block * block, axis=-1, keepdims=True) + EPSILON)
+        tk[0, h, core] = (block * scale).astype(jnp.bfloat16)
+        send(("core", 0, h), tk.at[0, h, core], tk.at[0, h, core], peer(0, False))
+    for h in range(2):
+        send(("link", 1, h), tk.at[0, h, core], tk.at[1, h, core], peer(1))
+    outw[me] = ow_ref[...].reshape(outw.shape[1:])
+
+    def store(tile, value, x, c, h):
+        if tile < 2:
+            value = value / (1.0 + jnp.exp(-value))
+        qkvb[x, c, pl.ds(h * half, half), pl.ds(tile * wide, wide)] = value.astype(jnp.bfloat16)
+
+    def project(relation, last=False):
+        chip = peer(relation) // 2
+        at = pl.multiple_of(chip * 2 * depth, 2 * depth)
+        left = tk[0, :, :, :, pl.ds(at, 2 * depth)].reshape(2 * rows, 2 * depth)
+        for tile in range(3):
+            span = pl.ds(tile * wide, wide)
+            right = wbuf[pl.ds(2 * chip, 2), :, span].reshape(2 * depth, wide)
+            value = jnp.dot(left, right, preferred_element_type=jnp.float32)
+            if relation > 0:
+                value += acc[:, span]
+            if not last:
+                acc[:, span] = value
+                continue
+            for h in range(2):
+                for c in range(2):
+                    k = h * 2 + c
+                    store(tile, value[k * half : (k + 1) * half], chip_x, c, h)
+
+    arrived("w", 0)
+    arrived("core", 0, 0)
+    arrived("core", 0, 1)
+    project(0)
+    for same in (True, False):
+        arrived("w", 1, same)
+        slot = wbuf.at[peer(1, same)]
+        send(("w", 3, same), slot, slot, peer(2))
+    project(1)
+    for same in (True, False):
+        arrived("w", 2, same)
+    project(2)
+    arrived("link", 1, 0)
+    send(("core", 1, 0), tk.at[1, 0, core], tk.at[1, 0, core], peer(0, False))
+    for same in (True, False):
+        arrived("w", 3, same)
+    send(("o", 0), outw.at[me], outw.at[me], peer(0, False))
+    for h in range(2):
+        send(("o", 2, 1 - h), outw.at[me, 1 - h], outw.at[me, 1 - h], peer(2))
+        send(("o", 1, h), outw.at[me, h], outw.at[me, h], peer(1))
+    project(3, last=True)
+    for h in range(2):
+        if h == 1:
+            arrived("link", 1, 1)
+            send(("core", 1, 1), tk.at[1, 1, core], tk.at[1, 1, core], peer(0, False))
+        arrived("core", 1, h)
+        left = tk[1, h].reshape(rows, width)
+        for tile in range(3):
+            right = wbuf[:, :, pl.ds(tile * wide, wide)].reshape(width, wide)
+            value = jnp.dot(left, right, preferred_element_type=jnp.float32)
+            for c in range(2):
+                store(tile, value[c * half : (c + 1) * half], 1 - chip_x, c, h)
+
+    def part(j, kind, head):
+        return qkvb[j // 2, j % 2, :, pl.ds(kind * wide + head * HD, HD)]
+
+    for head in range(2):
+        total = jnp.zeros((HD, HD), jnp.float32)
+        for j in range(4):
+            state = lax.dot_general(
+                part(j, 1, head), part(j, 2, head), (((0,), (0,)), ((), ())),
+                preferred_element_type=jnp.float32,
+            )
+            sbuf[j, head] = state
+            total += state
+        tsend[head] = total
+    send(("t",), tsend, trecv, peer(2))
+
+    def pass_out(relation, h):
+        slot = outw.at[peer(relation), h]
+        send(("oc", relation, h), slot, slot, peer(0, False))
+
+    arrived("o", 1, 0)
+    send(("o", 3, 0), outw.at[peer(1), 0], outw.at[peer(1), 0], peer(2))
+    pass_out(1, 0)
+    arrived("o", 2, 1)
+    send(("o", 3, 1), outw.at[peer(2), 1], outw.at[peer(2), 1], peer(1))
+    pass_out(2, 1)
+    causal = lax.broadcasted_iota(jnp.int32, (rows, rows), 0) >= lax.broadcasted_iota(
+        jnp.int32, (rows, rows), 1
+    )
+    for j in range(4):
+        for head in range(2):
+            scores = lax.dot_general(
+                part(j, 0, head), part(j, 1, head), (((1,), (1,)), ((), ())),
+                preferred_element_type=jnp.float32,
+            )
+            scores = jnp.where(causal, scores, 0.0).astype(jnp.bfloat16)
+            mixed[j, head] = jnp.dot(
+                scores, part(j, 2, head), preferred_element_type=jnp.float32
+            )
+    arrived("t")
+    later = (chip_y > 0).astype(jnp.float32)
+    for head in range(2):
+        carried = prior_ref[group * 2 + head] + trecv[head] * later
+        for j in range(4):
+            high = carried.astype(jnp.bfloat16)
+            low = (carried - high.astype(jnp.float32)).astype(jnp.bfloat16)
+            queries = part(j, 0, head)
+            total = (
+                mixed[j, head]
+                + jnp.dot(queries, high, preferred_element_type=jnp.float32)
+                + jnp.dot(queries, low, preferred_element_type=jnp.float32)
+            )
+            scale = lax.rsqrt(jnp.mean(total * total, axis=-1, keepdims=True) + EPSILON)
+            hnbuf[j, :, pl.ds(head * HD, HD)] = (total * scale).astype(jnp.bfloat16)
+            carried = carried + sbuf[j, head]
+    for relation, same in ((1, True), (1, False), (0, False)):
+        there = peer(relation, same)
+        send(("h", relation, same), hnbuf.at[there % 4], hall.at[group], there)
+    hall[group] = hnbuf[group]
+    arrived("o", 1, 1)
+    pass_out(1, 1)
+    arrived("o", 2, 0)
+    pass_out(2, 0)
+    for h in range(2):
+        arrived("o", 3, h)
+        pass_out(3, h)
+    arrived("o", 0)
+    for relation, same in ((1, True), (1, False), (0, False)):
+        arrived("h", relation, same)
+    for relation in range(1, CHIPS):
+        for h in range(2):
+            arrived("oc", relation, h)
+
+    @pl.loop(0, width // TILE)
+    def _(n):
+        span = pl.ds(pl.multiple_of(n * TILE, TILE), TILE)
+        total = tokens_ref[:, span].astype(jnp.float32)
+        for g in range(4):
+            right = outw[2 * g : 2 * g + 2, :, :, span].reshape(wide, TILE)
+            total += jnp.dot(hall[g], right, preferred_element_type=jnp.float32)
+        hidden_ref[:, span] = total.astype(jnp.bfloat16)
+
+    for copy in copies.values():
+        copy.wait_send()
+
+
+def attention_fused(tokens, qkv_weight, out_weight, prior_state):
+    rows, width = tokens.shape
+    depth = qkv_weight.shape[0]
+    wide = 2 * HD
+    half = rows // 2
+    bf16, f32 = jnp.bfloat16, jnp.float32
+    split = qkv_weight.reshape(depth, 3, 4, wide).transpose(2, 0, 1, 3)
+    split = split.reshape(4, depth, 3 * wide)
+    vmem = pl.BlockSpec(memory_space=pltpu.VMEM)
+    copies = 40
+    return pl.pallas_call(
+        attention_kernel,
+        out_shape=jax.ShapeDtypeStruct((rows, width), bf16),
+        in_specs=[vmem] * 4,
+        out_specs=vmem,
+        scratch_shapes=[
+            pltpu.VMEM((2, 2, 2, half, width), bf16),
+            pltpu.VMEM((8, depth, 3 * wide), bf16),
+            pltpu.VMEM((2 * rows, 3 * wide), f32),
+            pltpu.VMEM((2, 2, rows, 3 * wide), bf16),
+            pltpu.VMEM((4, 2, HD, HD), f32),
+            pltpu.VMEM((2, HD, HD), f32),
+            pltpu.VMEM((2, HD, HD), f32),
+            pltpu.VMEM((4, 2, rows, HD), f32),
+            pltpu.VMEM((4, rows, wide), bf16),
+            pltpu.VMEM((4, rows, wide), bf16),
+            pltpu.VMEM((8, 2, out_weight.shape[0] // 2, width), bf16),
+            pltpu.SemaphoreType.DMA((copies,)),
+            pltpu.SemaphoreType.DMA((copies,)),
+        ],
+        compiler_params=pltpu.CompilerParams(
+            collective_id=0, has_side_effects=True, vmem_limit_bytes=50 * 1024 * 1024
+        ),
+        cost_estimate=pl.CostEstimate(
+            flops=2 * rows * width * 4 * HEADS * HD,
+            bytes_accessed=16 * rows * width,
+            transcendentals=0,
+        ),
+        name="attention",
+    )(tokens, split, out_weight, prior_state)
+
+
 def shards(
     tokens, qkv_weight, out_weight, prior_state, expert_ids, gate_weights, expert_in, expert_out
 ):
@@ -278,6 +520,11 @@
     experts = local_experts * groups
     top_count = expert_ids.shape[1]
     capacity = 3 * tok_rows * top_count // (2 * experts)
+    if groups == 8 and local_experts == 1:
+        named = expert_ids[None] == jnp.arange(experts, dtype=jnp.int32)[:, None, None]
+        gates = jnp.sum(jnp.where(named, gate_weights[None], 0.0), axis=2)
+        hidden = attention_fused(tokens, qkv_weight, out_weight, prior_state)
+        return moe_fused(hidden, gates, expert_in, expert_out)
     normed = rms_rows(tokens.astype(jnp.float32)).astype(jnp.bfloat16)
     columns = normed
     projected = jnp.dot(
@@ -317,10 +564,6 @@
         preferred_element_type=jnp.float32,
     )
     hidden = (tokens.astype(jnp.float32) + attended).astype(jnp.bfloat16)
-    if groups == 8 and local_experts == 1:
-        named = expert_ids[None] == jnp.arange(experts, dtype=jnp.int32)[:, None, None]
-        gates = jnp.sum(jnp.where(named, gate_weights[None], 0.0), axis=2)
-        return moe_fused(hidden, gates, expert_in, expert_out)
     moe_in = rms_rows(hidden.astype(jnp.float32)).astype(jnp.bfloat16)
     flat_ids = expert_ids.reshape(-1)
     onehot = (flat_ids[:, None] == jnp.arange(experts, dtype=jnp.int32)[None, :]).astype(jnp.int32)

time: 280 us -> 188 us (0.67)
  waiting for transfers between devices: 134 us -> 0 us
  Pallas kernels: 107 us -> 178 us
  matrix products: 16.8 us -> 0 us
  between operations: 13.2 us -> 0.06 us
  local copies, waits for them, and re-layouts: 2.6 us -> 9.01 us
  other arithmetic: 6.16 us -> 0.62 us
    all_gather x3 -> x0, waiting for transfers between devices: 132 us -> none  [the longest x1 75.3 us: shards(): lax.all_gather(qkv_weight, 'ctx', axis=0, tiled=True)]
    pallas_call x0 -> x1, Pallas kernels: none -> 71.5 us  [attention_fused(): pl.pallas_call(attention_kernel, out_shape=jax.ShapeDtypeStruct((rows, wi...]
    dot_general x5 -> x0, matrix products: 16.8 us -> none  [the longest x1 6.75 us: shards(): jnp.dot(columns, lax.all_gather(qkv_weight, 'ctx', axis=0, tiled=True), p...]
    reduce_sum x2 -> x0, other arithmetic: 3.64 us -> none  [the longest x1 2.13 us: prefix(): return jnp.sum(jnp.where(reached, everything.astype(x.dtype), 0.0), axis=0)]
  transfers between devices with their start and end apart: 3 -> 0, of which waited for: 3 -> 0; matrix products, arithmetic and copies ran while one was open for 4% -> 0% of each run, Pallas kernels for 0% -> 0%
where the time goes in v2:
time: 188 us
  Pallas kernels  178 us (95%)
  local copies, waits for them, and re-layouts  9.01 us (5%)
    pallas_call x1, Pallas kernels, moe_fused(): pl.pallas_call(moe_kernel, out_shape=jax.ShapeDtypeStruct((rows, width),...  107 us
    pallas_call x1, Pallas kernels, attention_fused(): pl.pallas_call(attention_kernel, out_shape=jax.ShapeDtypeStruct((rows, wi...  71.5 us
    unnamed x14, local copies, waits for them, and re-layouts  4.99 us

profile of v2, /device:TPU:0, one launch (start us, length us, event | category | flops | bytes accessed | tf_op | source)
XLA Modules:
  0.0 188.1 jit_solution(4174443809282341947)
XLA Ops:
  0.0 1.7 copy.20
  1.7 1.3 copy.21
  3.0 0.0 copy-start
  3.0 0.0 copy-start.1
  3.0 0.0 copy-start.2
  3.0 2.7 %copy.22.wsplit_ref = bf16[4,256,768]{2,1,0:T(8,128)(2,1)} copy(bf16[4,256,768]{1,2,0:T(8,128)(2,1)} %bitcast.4) | data formatting | bytes 3145728 | tf_op jit(solution)/shard_map/reshape | solution.py:477
  5.7 0.0 copy-done
  5.7 0.0 copy-done.1
  5.7 0.0 copy-done.2
  5.7 0.0 copy-start.4
  5.8 0.0 copy-start.5
  5.8 71.5 %attention.1.hidden_ref = bf16[256,2048]{1,0:T(8,128)(2,1)S(1)} custom-call(bf16[256,2048]{1,0:T(8,128)(2,1)S(1)} %copy-done, bf16[4,256,768]{2,1,0:T(8,128)(2,1)} %copy.22.wsplit_ref, bf16[128,2048]{1,0:T(8,128)(2,1)S(1)} %copy-done.1, f32[8,128,128]{2,1,0:T(8,128)S(1)} %copy-done.2), custom_call_target="tpu_custom_call" | custom-call | flops 4294967296 | bytes 8388608 | tf_op jit(solution)/shard_map/attention/pallas_call | solution.py:480
  77.3 0.0 copy-start.3
  77.3 1.0 copy-done.3
  78.3 0.0 copy-done.4
  78.3 0.0 copy-done.5
  78.3 0.6 select_reduce_fusion.gates_ref
  78.9 106.9 %moe.1 = bf16[256,2048]{1,0:T(8,128)(2,1)} custom-call(bf16[256,2048]{1,0:T(8,128)(2,1)} %copy-done.3, f32[8,256]{1,0:T(8,128)} %select_reduce_fusion.gates_ref, bf16[1,2048,2048]{2,1,0:T(8,128)(2,1)} %win_hbm.1, bf16[1,1024,2048]{2,1,0:T(8,128)(2,1)} %wout_hbm.1), custom_call_target="tpu_custom_call" | custom-call | flops 25769803776 | bytes 12582912 | tf_op jit(solution)/shard_map/moe/pallas_call | solution.py:239
  185.7 2.3 %copy.24 = bf16[256,2048]{1,0:T(8,128)(2,1)} copy(bf16[256,2048]{1,0:T(8,128)(2,1)} %moe.1) | data formatting | bytes 2097152
Async XLA Ops:
  3.0 2.7 %copy-start = (bf16[256,2048]{1,0:T(8,128)(2,1)S(1)}, bf16[256,2048]{1,0:T(8,128)(2,1)}, u32[]{:S(2)}) copy-start(bf16[256,2048]{1,0:T(8,128)(2,1)} %tokens_ref.1) | copy-start | bytes 3145732
  3.0 2.7 %copy-start.1 = (bf16[128,2048]{1,0:T(8,128)(2,1)S(1)}, bf16[128,2048]{1,0:T(8,128)(2,1)}, u32[]{:S(2)}) copy-start(bf16[128,2048]{1,0:T(8,128)(2,1)} %ow_ref.1) | copy-start | bytes 1572868
  3.0 2.7 %copy-start.2 = (f32[8,128,128]{2,1,0:T(8,128)S(1)}, f32[8,128,128]{2,1,0:T(8,128)}, u32[]{:S(2)}) copy-start(f32[8,128,128]{2,1,0:T(8,128)} %prior_ref.1) | copy-start | bytes 1572868
  5.7 72.5 %copy-start.4 = (f32[256,4]{0,1:T(4,128)S(1)}, f32[256,4]{0,1:T(4,128)}, u32[]{:S(2)}) copy-start(f32[256,4]{0,1:T(4,128)} %param.13) | copy-start | bytes 12292
  5.8 72.5 %copy-start.5 = (s32[256,4]{0,1:T(4,128)S(1)}, s32[256,4]{0,1:T(4,128)}, u32[]{:S(2)}) copy-start(s32[256,4]{0,1:T(4,128)} %param.12) | copy-start | bytes 12292
  77.3 1.0 copy-start.3

commit v3 on v2

--- a/solution.py
+++ b/solution.py
@@ -32,7 +32,7 @@
 
 def moe_kernel(
     hidden_ref, gates_ref, win_hbm, wout_hbm, out_ref,
-    xg, win, wout, gath, part, pair, sendb, final, mid,
+    xg, win, wout, gath, part, pair, sendb, final, diag, mid,
     send_sem, recv_sem, gsend, grecv, wsem,
 ):
     me = lax.axis_index("ctx")
@@ -86,15 +86,13 @@
         slot = xg.at[relation, h, core]
         send(("core", relation, h), slot, slot, peer(0, False))
 
-    def arrived(kind, relation, h):
-        copies[(kind, relation, h)].wait_recv()
+    def arrived(*name):
+        copies[name].wait_recv()
 
     own(1, 0)
     own(2, 1)
     across(0, 0)
     across(0, 1)
-    own(1, 1)
-    own(2, 0)
     gath[me] = gates_ref[...]
     gate_copies = []
     for k in range(1, 8):
@@ -165,51 +163,57 @@
             send(("pair", relation, h), part.at[relation, h, 1 - core], pair.at[relation, h],
                  peer(0, False))
 
-    def give(relation, halves):
-        for h in halves:
-            arrived("pair", relation, h)
-            sendb[relation - 1, h] = (
-                part[relation, h, core].astype(jnp.float32)
-                + pair[relation, h].astype(jnp.float32)
-            ).astype(jnp.bfloat16)
-            send(("sum", relation, h), sendb.at[relation - 1, h], final.at[relation - 1, h],
-                 peer(relation))
+    def give(relation, h, corner=None):
+        arrived("pair", relation, h)
+        total = part[relation, h, core].astype(jnp.float32) + pair[relation, h].astype(jnp.float32)
+        if corner is not None:
+            arrived("corner", corner)
+            total += diag[corner].astype(jnp.float32)
+        sendb[relation - 1, h] = total.astype(jnp.bfloat16)
+        source = sendb.at[relation - 1, h]
+        if relation == 3:
+            send(("corner", h), source, diag.at[h], peer(1 + h))
+        else:
+            send(("sum", relation, h), source, final.at[relation - 1, h], peer(relation))
 
     arrived("core", 0, 0)
-    arrived("core", 0, 1)
-    expert(0, (0, 1))
+    expert(0, (0,))
     arrived("link", 1, 0)
     send(("link", 3, 0), xg.at[1, 0, core], xg.at[3, 0, core], peer(2))
-    across(1, 0)
     arrived("link", 2, 1)
     send(("link", 3, 1), xg.at[2, 1, core], xg.at[3, 1, core], peer(1))
+    own(1, 1)
+    own(2, 0)
+    across(1, 0)
     across(2, 1)
+    arrived("core", 0, 1)
+    expert(0, (1,))
     arrived("core", 1, 0)
     expert(1, (0,))
     arrived("core", 2, 1)
     expert(2, (1,))
-    give(1, (0,))
+    give(1, 0)
+    arrived("link", 3, 0)
+    across(3, 0)
+    arrived("link", 3, 1)
+    across(3, 1)
+    arrived("core", 3, 0)
+    expert(3, (0,))
+    give(2, 1)
+    arrived("core", 3, 1)
+    expert(3, (1,))
+    give(3, 0)
     arrived("link", 1, 1)
     across(1, 1)
     arrived("link", 2, 0)
     across(2, 0)
-    give(2, (1,))
+    give(3, 1)
     arrived("core", 1, 1)
     expert(1, (1,))
     arrived("core", 2, 0)
     expert(2, (0,))
-    give(1, (1,))
-    arrived("link", 3, 0)
-    across(3, 0)
-    arrived("link", 3, 1)
-    across(3, 1)
-    give(2, (0,))
-    arrived("core", 3, 0)
-    expert(3, (0,))
-    arrived("core", 3, 1)
-    expert(3, (1,))
-    give(3, (0,))
-    give(3, (1,))
+    give(1, 1, corner=1)
+    give(2, 0, corner=0)
     for h in range(2):
         arrived("pair", 0, h)
         span = pl.ds(h * half, half)
@@ -218,7 +222,7 @@
             + part[0, h, core].astype(jnp.float32)
             + pair[0, h].astype(jnp.float32)
         )
-        for relation in range(1, CHIPS):
+        for relation in (1, 2):
             arrived("sum", relation, h)
             total += final[relation - 1, h].astype(jnp.float32)
         out_ref[span, :] = total.astype(jnp.bfloat16)
@@ -249,7 +253,8 @@
             pltpu.VMEM((CHIPS, 2, 2, half, width), bf16),
             pltpu.VMEM((CHIPS, 2, half, width), bf16),
             pltpu.VMEM((CHIPS - 1, 2, half, width), bf16),
-            pltpu.VMEM((CHIPS - 1, 2, half, width), bf16),
+            pltpu.VMEM((2, 2, half, width), bf16),
+            pltpu.VMEM((2, half, width), bf16),
             pltpu.VMEM((2 * rows, ff), bf16),
             pltpu.SemaphoreType.DMA((copies,)),
             pltpu.SemaphoreType.DMA((copies,)),
@@ -268,8 +273,8 @@
 
 
 def attention_kernel(
-    tokens_ref, wsplit_ref, ow_ref, prior_ref, hidden_ref,
-    tk, wbuf, acc, qkvb, sbuf, tsend, trecv, mixed, hnbuf, hall, outw,
+    tokens_ref, qkv_ref, ow_ref, prior_ref, hidden_ref,
+    wsplit_ref, tk, wbuf, acc, qkvb, sbuf, tsend, trecv, mixed, hnbuf, hall, outw,
     send_sem, recv_sem,
 ):
     me = lax.axis_index("ctx")
@@ -279,6 +284,9 @@
     rows, width = tokens_ref.shape
     half = rows // 2
     group = chip_x * 2 + core
+    plane_at = lax.axis_index("dp")
+    side = plane_at % 2
+    beside = plane_at + 1 - 2 * side
     wide = 2 * HD
     depth = wbuf.shape[1]
 
@@ -292,18 +300,26 @@
         pl.semaphore_signal(
             barrier, inc=1, device_id={"ctx": (me + k) % 8}, device_id_type=MESH
         )
-    pl.semaphore_wait(barrier, 7)
+    pl.semaphore_signal(
+        barrier, inc=1, device_id={"dp": beside, "ctx": me}, device_id_type=MESH
+    )
+    for g in range(4):
+        for kind in range(3):
+            wsplit_ref[g, :, pl.ds(kind * wide, wide)] = qkv_ref[
+                :, pl.ds((kind * 4 + g) * wide, wide)
+            ]
+    pl.semaphore_wait(barrier, 8)
 
     copies = {}
 
-    def send(name, source, target, device):
+    def send(name, source, target, device, plane=None):
         index = len(copies)
         copies[name] = pltpu.make_async_remote_copy(
             src_ref=source,
             dst_ref=target,
             send_sem=send_sem.at[index],
             recv_sem=recv_sem.at[index],
-            device_id={"ctx": device},
+            device_id={"ctx": device} if plane is None else {"dp": plane, "ctx": device},
             device_id_type=MESH,
         )
         copies[name].start()
@@ -366,9 +382,9 @@
     for same in (True, False):
         arrived("w", 3, same)
     send(("o", 0), outw.at[me], outw.at[me], peer(0, False))
+    send(("o", 1), outw.at[me, side], outw.at[me, side], peer(1))
     for h in range(2):
-        send(("o", 2, 1 - h), outw.at[me, 1 - h], outw.at[me, 1 - h], peer(2))
-        send(("o", 1, h), outw.at[me, h], outw.at[me, h], peer(1))
+        send(("o", 2, h), outw.at[me, h], outw.at[me, h], peer(2))
     project(3, last=True)
     for h in range(2):
         if h == 1:
@@ -397,16 +413,16 @@
         tsend[head] = total
     send(("t",), tsend, trecv, peer(2))
 
-    def pass_out(relation, h):
+    def pass_out(name, relation, h, planes):
         slot = outw.at[peer(relation), h]
-        send(("oc", relation, h), slot, slot, peer(0, False))
-
-    arrived("o", 1, 0)
-    send(("o", 3, 0), outw.at[peer(1), 0], outw.at[peer(1), 0], peer(2))
-    pass_out(1, 0)
-    arrived("o", 2, 1)
-    send(("o", 3, 1), outw.at[peer(2), 1], outw.at[peer(2), 1], peer(1))
-    pass_out(2, 1)
+        arrived(*name)
+        if planes:
+            send(("oz", relation), slot, slot, me, beside)
+        send(("oc",) + name, slot, slot, peer(0, False))
+
+    pass_out(("o", 1), 1, side, True)
+    slot_x = outw.at[peer(1), side]
+    send(("o", 3), slot_x, slot_x, peer(2))
     causal = lax.broadcasted_iota(jnp.int32, (rows, rows), 0) >= lax.broadcasted_iota(
         jnp.int32, (rows, rows), 1
     )
@@ -420,6 +436,7 @@
             mixed[j, head] = jnp.dot(
                 scores, part(j, 2, head), preferred_element_type=jnp.float32
             )
+    pass_out(("o", 2, 0), 2, 0, False)
     arrived("t")
     later = (chip_y > 0).astype(jnp.float32)
     for head in range(2):
@@ -440,19 +457,15 @@
         there = peer(relation, same)
         send(("h", relation, same), hnbuf.at[there % 4], hall.at[group], there)
     hall[group] = hnbuf[group]
-    arrived("o", 1, 1)
-    pass_out(1, 1)
-    arrived("o", 2, 0)
-    pass_out(2, 0)
-    for h in range(2):
-        arrived("o", 3, h)
-        pass_out(3, h)
+    pass_out(("oz", 1), 1, 1 - side, False)
+    pass_out(("o", 2, 1), 2, 1, False)
+    pass_out(("o", 3), 3, side, True)
+    pass_out(("oz", 3), 3, 1 - side, False)
     arrived("o", 0)
     for relation, same in ((1, True), (1, False), (0, False)):
         arrived("h", relation, same)
-    for relation in range(1, CHIPS):
-        for h in range(2):
-            arrived("oc", relation, h)
+    for name in (("o", 1), ("o", 2, 0), ("oz", 1), ("o", 2, 1), ("o", 3), ("oz", 3)):
+        arrived("oc", *name)
 
     @pl.loop(0, width // TILE)
     def _(n):
@@ -473,8 +486,6 @@
     wide = 2 * HD
     half = rows // 2
     bf16, f32 = jnp.bfloat16, jnp.float32
-    split = qkv_weight.reshape(depth, 3, 4, wide).transpose(2, 0, 1, 3)
-    split = split.reshape(4, depth, 3 * wide)
     vmem = pl.BlockSpec(memory_space=pltpu.VMEM)
     copies = 40
     return pl.pallas_call(
@@ -483,6 +494,7 @@
         in_specs=[vmem] * 4,
         out_specs=vmem,
         scratch_shapes=[
+            pltpu.VMEM((4, depth, 3 * wide), bf16),
             pltpu.VMEM((2, 2, 2, half, width), bf16),
             pltpu.VMEM((8, depth, 3 * wide), bf16),
             pltpu.VMEM((2 * rows, 3 * wide), f32),
@@ -506,7 +518,7 @@
             transcendentals=0,
         ),
         name="attention",
-    )(tokens, split, out_weight, prior_state)
+    )(tokens, qkv_weight, out_weight, prior_state)
 
 
 def shards(
@@ -520,7 +532,7 @@
     experts = local_experts * groups
     top_count = expert_ids.shape[1]
     capacity = 3 * tok_rows * top_count // (2 * experts)
-    if groups == 8 and local_experts == 1:
+    if groups == 8 and local_experts == 1 and lax.axis_size("dp") % 2 == 0:
         named = expert_ids[None] == jnp.arange(experts, dtype=jnp.int32)[:, None, None]
         gates = jnp.sum(jnp.where(named, gate_weights[None], 0.0), axis=2)
         hidden = attention_fused(tokens, qkv_weight, out_weight, prior_state)

time: 188 us -> 170 us (0.904)
  Pallas kernels: 178 us -> 162 us
  local copies, waits for them, and re-layouts: 9.01 us -> 6.58 us
    pallas_call x1, Pallas kernels: 107 us -> 89.4 us  [moe_fused(): pl.pallas_call(moe_kernel, out_shape=jax.ShapeDtypeStruct((rows, width),...]
    reshape x1 -> x0, local copies, waits for them, and re-layouts: 2.74 us -> none  [attention_fused(): split = split.reshape(4, depth, 3 * wide)]
    unnamed x14 -> x9, local copies, waits for them, and re-layouts: 4.99 us -> 6.58 us
where the time goes in v3:
time: 170 us
  Pallas kernels  162 us (95%)
  local copies, waits for them, and re-layouts  6.58 us (4%)
    pallas_call x1, Pallas kernels, moe_fused(): pl.pallas_call(moe_kernel, out_shape=jax.ShapeDtypeStruct((rows, width),...  89.4 us
    pallas_call x1, Pallas kernels, attention_fused(): pl.pallas_call(attention_kernel, out_shape=jax.ShapeDtypeStruct((rows, wi...  72.8 us
    unnamed x9, local copies, waits for them, and re-layouts  6.58 us

profile of v3, /device:TPU:0, one launch (start us, length us, event | category | flops | bytes accessed | tf_op | source)
XLA Modules:
  0.0 170.1 jit_solution(10557722212742007960)
XLA Ops:
  0.0 1.3 select_reduce_fusion.gates_ref
  1.3 0.0 copy-start
  1.3 1.2 copy-done
  2.5 0.0 copy-start.1
  2.5 1.0 copy-done.1
  3.6 0.0 copy-start.2
  3.6 1.0 copy-done.2
  4.6 72.8 %attention.1.hidden_ref = bf16[256,2048]{1,0:T(8,128)(2,1)S(1)} custom-call(bf16[256,2048]{1,0:T(8,128)(2,1)S(1)} %copy-done, bf16[256,3072]{1,0:T(8,128)(2,1)} %qkv_ref.1, bf16[128,2048]{1,0:T(8,128)(2,1)S(1)} %copy-done.1, f32[8,128,128]{2,1,0:T(8,128)S(1)} %copy-done.2), custom_call_target="tpu_custom_call" | custom-call | flops 4294967296 | bytes 8388608 | tf_op jit(solution)/shard_map/attention/pallas_call | solution.py:491
  77.4 0.0 copy-start.3
  77.4 1.0 copy-done.3
  78.4 89.4 %moe.1 = bf16[256,2048]{1,0:T(8,128)(2,1)} custom-call(bf16[256,2048]{1,0:T(8,128)(2,1)} %copy-done.3, f32[8,256]{1,0:T(8,128)} %select_reduce_fusion.gates_ref, bf16[1,2048,2048]{2,1,0:T(8,128)(2,1)} %win_hbm.1, bf16[1,1024,2048]{2,1,0:T(8,128)(2,1)} %wout_hbm.1), custom_call_target="tpu_custom_call" | custom-call | flops 25769803776 | bytes 12582912 | tf_op jit(solution)/shard_map/moe/pallas_call | solution.py:243
  167.8 2.3 %copy.12 = bf16[256,2048]{1,0:T(8,128)(2,1)} copy(bf16[256,2048]{1,0:T(8,128)(2,1)} %moe.1) | data formatting | bytes 2097152
Async XLA Ops:
  1.3 1.2 copy-start
  2.5 1.0 copy-start.1
  3.6 1.0 copy-start.2
  77.4 1.0 copy-start.3

commit v4 on v3

--- a/solution.py
+++ b/solution.py
@@ -31,8 +31,8 @@
 
 
 def moe_kernel(
-    hidden_ref, gates_ref, win_hbm, wout_hbm, out_ref,
-    xg, win, wout, gath, part, pair, sendb, final, diag, mid,
+    hidden_ref, ids_ref, weights_ref, win_hbm, wout_hbm, out_ref,
+    gates_ref, xg, win, wout, gath, part, pair, sendb, final, diag, mid,
     send_sem, recv_sem, gsend, grecv, wsem,
 ):
     me = lax.axis_index("ctx")
@@ -59,6 +59,12 @@
     load_in.start()
     load_out.start()
 
+    gates_ref[...] = jnp.zeros_like(gates_ref)
+    expert_at = lax.broadcasted_iota(jnp.int32, gates_ref.shape, 0)
+    for k in range(ids_ref.shape[0]):
+        gates_ref[...] += jnp.where(
+            expert_at == ids_ref[k : k + 1, :], weights_ref[k : k + 1, :], 0.0
+        )
     for h in range(2):
         block = hidden_ref[pl.ds(h * half, half), :].astype(jnp.float32)
         scale = lax.rsqrt(jnp.mean(block * block, axis=-1, keepdims=True) + EPSILON)
@@ -225,14 +231,14 @@
         for relation in (1, 2):
             arrived("sum", relation, h)
             total += final[relation - 1, h].astype(jnp.float32)
-        out_ref[span, :] = total.astype(jnp.bfloat16)
+        out_ref[span, :] = total
     for copy in gate_copies:
         copy.wait_send()
     for copy in copies.values():
         copy.wait_send()
 
 
-def moe_fused(hidden, gates, expert_in, expert_out):
+def moe_fused(hidden, ids, weights, expert_in, expert_out):
     rows, width = hidden.shape
     ff = expert_out.shape[1]
     half = rows // 2
@@ -242,14 +248,15 @@
     copies = 34
     return pl.pallas_call(
         moe_kernel,
-        out_shape=jax.ShapeDtypeStruct((rows, width), bf16),
-        in_specs=[vmem, vmem, hbm, hbm],
+        out_shape=jax.ShapeDtypeStruct((rows, width), jnp.float32),
+        in_specs=[vmem, vmem, vmem, hbm, hbm],
         out_specs=vmem,
         scratch_shapes=[
+            pltpu.VMEM((8, rows), jnp.float32),
             pltpu.VMEM((CHIPS, 2, 2, half, width), bf16),
             pltpu.VMEM(expert_in.shape[1:], bf16),
             pltpu.VMEM(expert_out.shape[1:], bf16),
-            pltpu.VMEM((8,) + gates.shape, jnp.float32),
+            pltpu.VMEM((8, 8, rows), jnp.float32),
             pltpu.VMEM((CHIPS, 2, 2, half, width), bf16),
             pltpu.VMEM((CHIPS, 2, half, width), bf16),
             pltpu.VMEM((CHIPS - 1, 2, half, width), bf16),
@@ -263,19 +270,19 @@
             pltpu.SemaphoreType.DMA((2,)),
         ],
         compiler_params=pltpu.CompilerParams(
-            collective_id=1, has_side_effects=True, vmem_limit_bytes=58 * 1024 * 1024
+            collective_id=1, has_side_effects=True, vmem_limit_bytes=60 * 1024 * 1024
         ),
         cost_estimate=pl.CostEstimate(
             flops=6 * 8 * rows * width * ff, bytes_accessed=6 * width * ff, transcendentals=0
         ),
         name="moe",
-    )(hidden, gates, expert_in, expert_out)
+    )(hidden, ids, weights, expert_in, expert_out)
 
 
 def attention_kernel(
-    tokens_ref, qkv_ref, ow_ref, prior_ref, hidden_ref,
-    wsplit_ref, tk, wbuf, acc, qkvb, sbuf, tsend, trecv, mixed, hnbuf, hall, outw,
-    send_sem, recv_sem,
+    tokens_hbm, qkv_hbm, ow_hbm, prior_hbm, hidden_ref,
+    tokens_ref, prior_ref, wsplit_ref, tk, wbuf, acc, qkvb, sbuf, tsend, trecv, mixed, hnbuf, hall, outw,
+    send_sem, recv_sem, local_sem,
 ):
     me = lax.axis_index("ctx")
     core = me % 2
@@ -303,11 +310,25 @@
     pl.semaphore_signal(
         barrier, inc=1, device_id={"dp": beside, "ctx": me}, device_id_type=MESH
     )
+    loads = []
+
+    def load(source, target):
+        loads.append(pltpu.make_async_copy(source, target, local_sem.at[len(loads)]))
+        loads[-1].start()
+
     for g in range(4):
         for kind in range(3):
-            wsplit_ref[g, :, pl.ds(kind * wide, wide)] = qkv_ref[
-                :, pl.ds((kind * 4 + g) * wide, wide)
-            ]
+            load(
+                qkv_hbm.at[:, pl.ds((kind * 4 + g) * wide, wide)],
+                wsplit_ref.at[g, :, pl.ds(kind * wide, wide)],
+            )
+    load(tokens_hbm, tokens_ref)
+    load(prior_hbm.at[pl.ds(group * 2, 2)], prior_ref)
+    strip = outw.shape[2]
+    for h in range(2):
+        load(ow_hbm.at[pl.ds(h * strip, strip)], outw.at[me, h])
+    for copy in loads[:12]:
+        copy.wait()
     pl.semaphore_wait(barrier, 8)
 
     copies = {}
@@ -327,11 +348,24 @@
     def arrived(*name):
         copies[name].wait_recv()
 
+    hd = depth // 2
+    mine = pl.ds(side * hd, hd)
+
+    def own_weights(k):
+        for same in (True, False):
+            other = core if same else 1 - core
+            span = pl.ds(k * hd, hd)
+            send(("w", 2, same, k), wsplit_ref.at[chip_x * 2 + other, span], wbuf.at[me, span],
+                 peer(2, same))
+
     for same in (True, False):
         other = core if same else 1 - core
-        send(("w", 1, same), wsplit_ref.at[(1 - chip_x) * 2 + other], wbuf.at[me], peer(1, same))
-        send(("w", 2, same), wsplit_ref.at[chip_x * 2 + other], wbuf.at[me], peer(2, same))
+        send(("w", 1, same), wsplit_ref.at[(1 - chip_x) * 2 + other, mine], wbuf.at[me, mine],
+             peer(1, same))
+    own_weights(0)
     send(("w", 0), wsplit_ref.at[chip_x * 2 + 1 - core], wbuf.at[me], peer(0, False))
+    for copy in loads[12:]:
+        copy.wait()
     wbuf[me] = wsplit_ref[group]
     for h in range(2):
         block = tokens_ref[pl.ds(h * half, half), :].astype(jnp.float32)
@@ -340,12 +374,11 @@
         send(("core", 0, h), tk.at[0, h, core], tk.at[0, h, core], peer(0, False))
     for h in range(2):
         send(("link", 1, h), tk.at[0, h, core], tk.at[1, h, core], peer(1))
-    outw[me] = ow_ref[...].reshape(outw.shape[1:])
-
-    def store(tile, value, x, c, h):
+
+    def store(tile, value, relation, c, h):
         if tile < 2:
             value = value / (1.0 + jnp.exp(-value))
-        qkvb[x, c, pl.ds(h * half, half), pl.ds(tile * wide, wide)] = value.astype(jnp.bfloat16)
+        qkvb[relation, c, pl.ds(h * half, half), pl.ds(tile * wide, wide)] = value.astype(jnp.bfloat16)
 
     def project(relation, last=False):
         chip = peer(relation) // 2
@@ -363,7 +396,7 @@
             for h in range(2):
                 for c in range(2):
                     k = h * 2 + c
-                    store(tile, value[k * half : (k + 1) * half], chip_x, c, h)
+                    store(tile, value[k * half : (k + 1) * half], 0, c, h)
 
     arrived("w", 0)
     arrived("core", 0, 0)
@@ -371,46 +404,78 @@
     project(0)
     for same in (True, False):
         arrived("w", 1, same)
-        slot = wbuf.at[peer(1, same)]
+        slot = wbuf.at[peer(1, same), mine]
         send(("w", 3, same), slot, slot, peer(2))
+        send(("wz", 1, same), slot, slot, me, beside)
+    own_weights(1)
+    for same in (True, False):
+        arrived("wz", 1, same)
     project(1)
     for same in (True, False):
-        arrived("w", 2, same)
-    project(2)
+        arrived("w", 3, same)
+        slot = wbuf.at[peer(3, same), mine]
+        send(("wz", 3, same), slot, slot, me, beside)
     arrived("link", 1, 0)
     send(("core", 1, 0), tk.at[1, 0, core], tk.at[1, 0, core], peer(0, False))
-    for same in (True, False):
-        arrived("w", 3, same)
+    for k in range(2):
+        for same in (True, False):
+            arrived("w", 2, same, k)
     send(("o", 0), outw.at[me], outw.at[me], peer(0, False))
-    send(("o", 1), outw.at[me, side], outw.at[me, side], peer(1))
     for h in range(2):
         send(("o", 2, h), outw.at[me, h], outw.at[me, h], peer(2))
+    project(2)
+    for same in (True, False):
+        arrived("wz", 3, same)
     project(3, last=True)
-    for h in range(2):
-        if h == 1:
-            arrived("link", 1, 1)
-            send(("core", 1, 1), tk.at[1, 1, core], tk.at[1, 1, core], peer(0, False))
+
+    def part(relation, c, kind, head):
+        return qkvb[relation, c, :, pl.ds(kind * wide + head * HD, HD)]
+
+    def states(relation):
+        for head in range(2):
+            for c in range(2):
+                sbuf[relation, c, head] = lax.dot_general(
+                    part(relation, c, 1, head), part(relation, c, 2, head),
+                    (((0,), (0,)), ((), ())), preferred_element_type=jnp.float32,
+                )
+
+    causal = lax.broadcasted_iota(jnp.int32, (rows, rows), 0) >= lax.broadcasted_iota(
+        jnp.int32, (rows, rows), 1
+    )
+
+    def inside(relation):
+        for head in range(2):
+            for c in range(2):
+                scores = lax.dot_general(
+                    part(relation, c, 0, head), part(relation, c, 1, head),
+                    (((1,), (1,)), ((), ())), preferred_element_type=jnp.float32,
+                )
+                scores = jnp.where(causal, scores, 0.0).astype(jnp.bfloat16)
+                mixed[relation, c, head] = jnp.dot(
+                    scores, part(relation, c, 2, head), preferred_element_type=jnp.float32
+                )
+
+    def project_other(h):
         arrived("core", 1, h)
         left = tk[1, h].reshape(rows, width)
         for tile in range(3):
             right = wbuf[:, :, pl.ds(tile * wide, wide)].reshape(width, wide)
             value = jnp.dot(left, right, preferred_element_type=jnp.float32)
             for c in range(2):
-                store(tile, value[c * half : (c + 1) * half], 1 - chip_x, c, h)
-
-    def part(j, kind, head):
-        return qkvb[j // 2, j % 2, :, pl.ds(kind * wide + head * HD, HD)]
-
+                store(tile, value[c * half : (c + 1) * half], 1, c, h)
+
+    project_other(0)
+    states(0)
+    arrived("link", 1, 1)
+    send(("core", 1, 1), tk.at[1, 1, core], tk.at[1, 1, core], peer(0, False))
+    send(("o", 1), outw.at[me, side], outw.at[me, side], peer(1))
+    inside(0)
+    project_other(1)
+    states(1)
     for head in range(2):
-        total = jnp.zeros((HD, HD), jnp.float32)
-        for j in range(4):
-            state = lax.dot_general(
-                part(j, 1, head), part(j, 2, head), (((0,), (0,)), ((), ())),
-                preferred_element_type=jnp.float32,
-            )
-            sbuf[j, head] = state
-            total += state
-        tsend[head] = total
+        tsend[head] = (sbuf[0, 0, head] + sbuf[0, 1, head]) + (
+            sbuf[1, 0, head] + sbuf[1, 1, head]
+        )
     send(("t",), tsend, trecv, peer(2))
 
     def pass_out(name, relation, h, planes):
@@ -423,40 +488,34 @@
     pass_out(("o", 1), 1, side, True)
     slot_x = outw.at[peer(1), side]
     send(("o", 3), slot_x, slot_x, peer(2))
-    causal = lax.broadcasted_iota(jnp.int32, (rows, rows), 0) >= lax.broadcasted_iota(
-        jnp.int32, (rows, rows), 1
-    )
-    for j in range(4):
-        for head in range(2):
-            scores = lax.dot_general(
-                part(j, 0, head), part(j, 1, head), (((1,), (1,)), ((), ())),
-                preferred_element_type=jnp.float32,
-            )
-            scores = jnp.where(causal, scores, 0.0).astype(jnp.bfloat16)
-            mixed[j, head] = jnp.dot(
-                scores, part(j, 2, head), preferred_element_type=jnp.float32
-            )
+    inside(1)
     pass_out(("o", 2, 0), 2, 0, False)
     arrived("t")
     later = (chip_y > 0).astype(jnp.float32)
-    for head in range(2):
-        carried = prior_ref[group * 2 + head] + trecv[head] * later
-        for j in range(4):
-            high = carried.astype(jnp.bfloat16)
-            low = (carried - high.astype(jnp.float32)).astype(jnp.bfloat16)
-            queries = part(j, 0, head)
-            total = (
-                mixed[j, head]
-                + jnp.dot(queries, high, preferred_element_type=jnp.float32)
-                + jnp.dot(queries, low, preferred_element_type=jnp.float32)
-            )
-            scale = lax.rsqrt(jnp.mean(total * total, axis=-1, keepdims=True) + EPSILON)
-            hnbuf[j, :, pl.ds(head * HD, HD)] = (total * scale).astype(jnp.bfloat16)
-            carried = carried + sbuf[j, head]
-    for relation, same in ((1, True), (1, False), (0, False)):
-        there = peer(relation, same)
-        send(("h", relation, same), hnbuf.at[there % 4], hall.at[group], there)
-    hall[group] = hnbuf[group]
+    for relation in (1, 0):
+        first = chip_x if relation == 0 else 1 - chip_x
+        for c in range(2):
+            for head in range(2):
+                carried = prior_ref[head] + trecv[head] * later
+                ahead = sbuf[1 - relation, 0, head] + sbuf[1 - relation, 1, head]
+                carried += ahead * (first > 0).astype(jnp.float32)
+                if c:
+                    carried += sbuf[relation, 0, head]
+                high = carried.astype(jnp.bfloat16)
+                low = (carried - high.astype(jnp.float32)).astype(jnp.bfloat16)
+                queries = part(relation, c, 0, head)
+                total = (
+                    mixed[relation, c, head]
+                    + jnp.dot(queries, high, preferred_element_type=jnp.float32)
+                    + jnp.dot(queries, low, preferred_element_type=jnp.float32)
+                )
+                scale = lax.rsqrt(jnp.mean(total * total, axis=-1, keepdims=True) + EPSILON)
+                hnbuf[relation, c, :, pl.ds(head * HD, HD)] = (total * scale).astype(jnp.bfloat16)
+        for same in (True, False)[1 - relation :]:
+            other = core if same else 1 - core
+            send(("h", relation, same), hnbuf.at[relation, other], hall.at[group],
+                 peer(relation, same))
+    hall[group] = hnbuf[0, core]
     pass_out(("oz", 1), 1, 1 - side, False)
     pass_out(("o", 2, 1), 2, 1, False)
     pass_out(("o", 3), 3, side, True)
@@ -491,23 +550,26 @@
     return pl.pallas_call(
         attention_kernel,
         out_shape=jax.ShapeDtypeStruct((rows, width), bf16),
-        in_specs=[vmem] * 4,
+        in_specs=[pl.BlockSpec(memory_space=pl.ANY)] * 4,
         out_specs=vmem,
         scratch_shapes=[
+            pltpu.VMEM((rows, width), bf16),
+            pltpu.VMEM((2, HD, HD), f32),
             pltpu.VMEM((4, depth, 3 * wide), bf16),
             pltpu.VMEM((2, 2, 2, half, width), bf16),
             pltpu.VMEM((8, depth, 3 * wide), bf16),
             pltpu.VMEM((2 * rows, 3 * wide), f32),
             pltpu.VMEM((2, 2, rows, 3 * wide), bf16),
-            pltpu.VMEM((4, 2, HD, HD), f32),
+            pltpu.VMEM((2, 2, 2, HD, HD), f32),
             pltpu.VMEM((2, HD, HD), f32),
             pltpu.VMEM((2, HD, HD), f32),
-            pltpu.VMEM((4, 2, rows, HD), f32),
-            pltpu.VMEM((4, rows, wide), bf16),
+            pltpu.VMEM((2, 2, 2, rows, HD), f32),
+            pltpu.VMEM((2, 2, rows, wide), bf16),
             pltpu.VMEM((4, rows, wide), bf16),
             pltpu.VMEM((8, 2, out_weight.shape[0] // 2, width), bf16),
             pltpu.SemaphoreType.DMA((copies,)),
             pltpu.SemaphoreType.DMA((copies,)),
+            pltpu.SemaphoreType.DMA((16,)),
         ],
         compiler_params=pltpu.CompilerParams(
             collective_id=0, has_side_effects=True, vmem_limit_bytes=50 * 1024 * 1024
@@ -533,10 +595,10 @@
     top_count = expert_ids.shape[1]
     capacity = 3 * tok_rows * top_count // (2 * experts)
     if groups == 8 and local_experts == 1 and lax.axis_size("dp") % 2 == 0:
-        named = expert_ids[None] == jnp.arange(experts, dtype=jnp.int32)[:, None, None]
-        gates = jnp.sum(jnp.where(named, gate_weights[None], 0.0), axis=2)
         hidden = attention_fused(tokens, qkv_weight, out_weight, prior_state)
-        return moe_fused(hidden, gates, expert_in, expert_out)
+        return moe_fused(hidden, expert_ids.T, gate_weights.T, expert_in, expert_out).astype(
+            jnp.bfloat16
+        )
     normed = rms_rows(tokens.astype(jnp.float32)).astype(jnp.bfloat16)
     columns = normed
     projected = jnp.dot(

time: 170 us -> 162 us (0.953)
  Pallas kernels: 162 us -> 154 us
  local copies, waits for them, and re-layouts: 6.58 us -> 4.27 us
    pallas_call x1, Pallas kernels: 72.8 us -> 64.8 us  [attention_fused(): pl.pallas_call(attention_kernel, out_shape=jax.ShapeDtypeStruct((rows, wi...]
    convert_element_type x0 -> x1, other arithmetic: none -> 2.71 us  [shards(): moe_fused(hidden, expert_ids.T, gate_weights.T, expert_in, expert_out)]
    unnamed x9 -> x8, local copies, waits for them, and re-layouts: 6.58 us -> 4.27 us
where the time goes in v4:
time: 162 us; the launch traced here: 161 us
  Pallas kernels  154 us (95%)
  local copies, waits for them, and re-layouts  4.27 us (3%)
  other arithmetic  2.71 us (2%)
    pallas_call x1, Pallas kernels, moe_fused(): pl.pallas_call(moe_kernel, out_shape=jax.ShapeDtypeStruct((rows, width),...  89.4 us
    pallas_call x1, Pallas kernels, attention_fused(): pl.pallas_call(attention_kernel, out_shape=jax.ShapeDtypeStruct((rows, wi...  64.8 us
    unnamed x8, local copies, waits for them, and re-layouts  4.27 us

profile of v4, /device:TPU:0, one launch (start us, length us, event | category | flops | bytes accessed | tf_op | source)
XLA Modules:
  0.0 161.3 jit_solution(12700302365298443563)
XLA Ops:
  0.0 0.0 copy-start
  0.0 1.2 copy-done
  1.2 0.0 copy-start.1
  1.2 1.0 copy-done.1
  2.3 0.0 copy-start.2
  2.3 1.0 copy-done.2
  3.3 64.8 %attention.1.hidden_ref = bf16[256,2048]{1,0:T(8,128)(2,1)S(1)} custom-call(bf16[256,2048]{1,0:T(8,128)(2,1)S(1)} %copy-done, bf16[256,3072]{1,0:T(8,128)(2,1)} %qkv_hbm.1, bf16[128,2048]{1,0:T(8,128)(2,1)S(1)} %copy-done.1, f32[8,128,128]{2,1,0:T(8,128)S(1)} %copy-done.2), custom_call_target="tpu_custom_call" | custom-call | flops 4294967296 | bytes 8388608 | tf_op jit(solution)/shard_map/attention/pallas_call | solution.py:550
  68.2 0.0 copy-start.3
  68.2 1.0 copy-done.3
  69.1 89.4 %moe.1 = f32[256,2048]{1,0:T(8,128)} custom-call(bf16[256,2048]{1,0:T(8,128)(2,1)} %copy-done.3, s32[4,256]{1,0:T(4,128)} %bitcast.2, f32[4,256]{1,0:T(4,128)} %bitcast.3, bf16[1,2048,2048]{2,1,0:T(8,128)(2,1)} %win_hbm.1, bf16[1,1024,2048]{2,1,0:T(8,128)(2,1)} %wout_hbm.1), custom_call_target="tpu_custom_call" | custom-call | flops 25769803776 | bytes 12582912 | tf_op jit(solution)/shard_map/moe/pallas_call | solution.py:249
  158.5 2.7 %convert_element_type.3 = bf16[256,2048]{1,0:T(8,128)(2,1)} convert(f32[256,2048]{1,0:T(8,128)} %moe.1) | non-fusion elementwise | flops 524288 | bytes 3145728 | tf_op jit(solution)/shard_map/convert_element_type | solution.py:599
Async XLA Ops:
  0.0 1.2 copy-start
  1.2 1.0 copy-start.1
  2.3 1.0 copy-start.2
  68.2 1.0 copy-start.3

commit v5 on v4

--- a/solution.py
+++ b/solution.py
@@ -188,32 +188,32 @@
     send(("link", 3, 0), xg.at[1, 0, core], xg.at[3, 0, core], peer(2))
     arrived("link", 2, 1)
     send(("link", 3, 1), xg.at[2, 1, core], xg.at[3, 1, core], peer(1))
-    own(1, 1)
-    own(2, 0)
     across(1, 0)
     across(2, 1)
     arrived("core", 0, 1)
     expert(0, (1,))
     arrived("core", 1, 0)
     expert(1, (0,))
+    own(1, 1)
+    own(2, 0)
     arrived("core", 2, 1)
     expert(2, (1,))
-    give(1, 0)
     arrived("link", 3, 0)
     across(3, 0)
     arrived("link", 3, 1)
     across(3, 1)
     arrived("core", 3, 0)
     expert(3, (0,))
-    give(2, 1)
     arrived("core", 3, 1)
     expert(3, (1,))
     give(3, 0)
+    give(3, 1)
+    give(1, 0)
+    give(2, 1)
     arrived("link", 1, 1)
     across(1, 1)
     arrived("link", 2, 0)
     across(2, 0)
-    give(3, 1)
     arrived("core", 1, 1)
     expert(1, (1,))
     arrived("core", 2, 0)
@@ -231,7 +231,7 @@
         for relation in (1, 2):
             arrived("sum", relation, h)
             total += final[relation - 1, h].astype(jnp.float32)
-        out_ref[span, :] = total
+        out_ref[span, :] = total.astype(jnp.bfloat16)
     for copy in gate_copies:
         copy.wait_send()
     for copy in copies.values():
@@ -248,7 +248,7 @@
     copies = 34
     return pl.pallas_call(
         moe_kernel,
-        out_shape=jax.ShapeDtypeStruct((rows, width), jnp.float32),
+        out_shape=jax.ShapeDtypeStruct((rows, width), bf16),
         in_specs=[vmem, vmem, vmem, hbm, hbm],
         out_specs=vmem,
         scratch_shapes=[
@@ -572,7 +572,7 @@
             pltpu.SemaphoreType.DMA((16,)),
         ],
         compiler_params=pltpu.CompilerParams(
-            collective_id=0, has_side_effects=True, vmem_limit_bytes=50 * 1024 * 1024
+            collective_id=0, has_side_effects=True, vmem_limit_bytes=60 * 1024 * 1024
         ),
         cost_estimate=pl.CostEstimate(
             flops=2 * rows * width * 4 * HEADS * HD,
@@ -596,9 +596,7 @@
     capacity = 3 * tok_rows * top_count // (2 * experts)
     if groups == 8 and local_experts == 1 and lax.axis_size("dp") % 2 == 0:
         hidden = attention_fused(tokens, qkv_weight, out_weight, prior_state)
-        return moe_fused(hidden, expert_ids.T, gate_weights.T, expert_in, expert_out).astype(
-            jnp.bfloat16
-        )
+        return moe_fused(hidden, expert_ids.T, gate_weights.T, expert_in, expert_out)
     normed = rms_rows(tokens.astype(jnp.float32)).astype(jnp.bfloat16)
     columns = normed
     projected = jnp.dot(

time: 162 us -> 162 us (level)
  Pallas kernels: 154 us -> 160 us
  other arithmetic: 2.71 us -> 0 us
  local copies, waits for them, and re-layouts: 4.27 us -> 2.3 us
    pallas_call x1, Pallas kernels: 89.4 us -> 94 us  [moe_fused(): pl.pallas_call(moe_kernel, out_shape=jax.ShapeDtypeStruct((rows, width),...]
    convert_element_type x1 -> x0, other arithmetic: 2.71 us -> none  [shards(): moe_fused(hidden, expert_ids.T, gate_weights.T, expert_in, expert_out)]
    unnamed x8 -> x1, local copies, waits for them, and re-layouts: 4.27 us -> 2.3 us
where the time goes in v5:
time: 162 us
  Pallas kernels  160 us (99%)
  local copies, waits for them, and re-layouts  2.3 us (1%)
    pallas_call x1, Pallas kernels, moe_fused(): pl.pallas_call(moe_kernel, out_shape=jax.ShapeDtypeStruct((rows, width),...  94 us
    pallas_call x1, Pallas kernels, attention_fused(): pl.pallas_call(attention_kernel, out_shape=jax.ShapeDtypeStruct((rows, wi...  65.8 us

profile of v5, /device:TPU:0, one launch (start us, length us, event | category | flops | bytes accessed | tf_op | source)
XLA Modules:
  0.0 162.2 jit_solution(3488817127406871165)
XLA Ops:
  0.0 65.8 %attention.1.hidden_ref = bf16[256,2048]{1,0:T(8,128)(2,1)} custom-call(bf16[256,2048]{1,0:T(8,128)(2,1)} %tokens_hbm.1, bf16[256,3072]{1,0:T(8,128)(2,1)} %qkv_hbm.1, bf16[128,2048]{1,0:T(8,128)(2,1)} %ow_hbm.1, f32[8,128,128]{2,1,0:T(8,128)} %prior_hbm.1), custom_call_target="tpu_custom_call" | custom-call | flops 4294967296 | bytes 8388608 | tf_op jit(solution)/shard_map/attention/pallas_call | solution.py:550
  65.9 94.0 %moe.1 = bf16[256,2048]{1,0:T(8,128)(2,1)} custom-call(bf16[256,2048]{1,0:T(8,128)(2,1)} %attention.1.hidden_ref, s32[4,256]{1,0:T(4,128)} %bitcast.2, f32[4,256]{1,0:T(4,128)} %bitcast.3, bf16[1,2048,2048]{2,1,0:T(8,128)(2,1)} %win_hbm.1, bf16[1,1024,2048]{2,1,0:T(8,128)(2,1)} %wout_hbm.1), custom_call_target="tpu_custom_call" | custom-call | flops 25769803776 | bytes 12582912 | tf_op jit(solution)/shard_map/moe/pallas_call | solution.py:249
  159.9 2.3 %copy.10 = bf16[256,2048]{1,0:T(8,128)(2,1)} copy(bf16[256,2048]{1,0:T(8,128)(2,1)} %moe.1) | data formatting | bytes 2097152

commit v6 on v5

--- a/solution.py
+++ b/solution.py
@@ -183,37 +183,35 @@
             send(("sum", relation, h), source, final.at[relation - 1, h], peer(relation))
 
     arrived("core", 0, 0)
-    expert(0, (0,))
+    arrived("core", 0, 1)
+    expert(0, (0, 1))
     arrived("link", 1, 0)
     send(("link", 3, 0), xg.at[1, 0, core], xg.at[3, 0, core], peer(2))
     arrived("link", 2, 1)
     send(("link", 3, 1), xg.at[2, 1, core], xg.at[3, 1, core], peer(1))
+    own(1, 1)
+    own(2, 0)
     across(1, 0)
     across(2, 1)
-    arrived("core", 0, 1)
-    expert(0, (1,))
     arrived("core", 1, 0)
     expert(1, (0,))
-    own(1, 1)
-    own(2, 0)
     arrived("core", 2, 1)
     expert(2, (1,))
+    give(1, 0)
     arrived("link", 3, 0)
     across(3, 0)
     arrived("link", 3, 1)
     across(3, 1)
+    give(2, 1)
     arrived("core", 3, 0)
-    expert(3, (0,))
     arrived("core", 3, 1)
-    expert(3, (1,))
-    give(3, 0)
-    give(3, 1)
-    give(1, 0)
-    give(2, 1)
+    expert(3, (0, 1))
     arrived("link", 1, 1)
     across(1, 1)
     arrived("link", 2, 0)
     across(2, 0)
+    give(3, 0)
+    give(3, 1)
     arrived("core", 1, 1)
     expert(1, (1,))
     arrived("core", 2, 0)

time: 162 us -> 157 us (0.969)
  Pallas kernels: 160 us -> 155 us
    pallas_call x1, Pallas kernels: 94 us -> 88.9 us  [moe_fused(): pl.pallas_call(moe_kernel, out_shape=jax.ShapeDtypeStruct((rows, width),...]
where the time goes in v6:
time: 157 us
  Pallas kernels  155 us (99%)
  local copies, waits for them, and re-layouts  2.3 us (1%)
    pallas_call x1, Pallas kernels, moe_fused(): pl.pallas_call(moe_kernel, out_shape=jax.ShapeDtypeStruct((rows, width),...  88.9 us
    pallas_call x1, Pallas kernels, attention_fused(): pl.pallas_call(attention_kernel, out_shape=jax.ShapeDtypeStruct((rows, wi...  65.8 us

profile of v6, /device:TPU:0, one launch (start us, length us, event | category | flops | bytes accessed | tf_op | source)
XLA Modules:
  0.0 157.1 jit_solution(6937448730227901893)
XLA Ops:
  0.0 65.8 %attention.1.hidden_ref = bf16[256,2048]{1,0:T(8,128)(2,1)} custom-call(bf16[256,2048]{1,0:T(8,128)(2,1)} %tokens_hbm.1, bf16[256,3072]{1,0:T(8,128)(2,1)} %qkv_hbm.1, bf16[128,2048]{1,0:T(8,128)(2,1)} %ow_hbm.1, f32[8,128,128]{2,1,0:T(8,128)} %prior_hbm.1), custom_call_target="tpu_custom_call" | custom-call | flops 4294967296 | bytes 8388608 | tf_op jit(solution)/shard_map/attention/pallas_call | solution.py:548
  65.9 88.9 %moe.1 = bf16[256,2048]{1,0:T(8,128)(2,1)} custom-call(bf16[256,2048]{1,0:T(8,128)(2,1)} %attention.1.hidden_ref, s32[4,256]{1,0:T(4,128)} %bitcast.2, f32[4,256]{1,0:T(4,128)} %bitcast.3, bf16[1,2048,2048]{2,1,0:T(8,128)(2,1)} %win_hbm.1, bf16[1,1024,2048]{2,1,0:T(8,128)(2,1)} %wout_hbm.1), custom_call_target="tpu_custom_call" | custom-call | flops 25769803776 | bytes 12582912 | tf_op jit(solution)/shard_map/moe/pallas_call | solution.py:247
  154.8 2.3 %copy.10 = bf16[256,2048]{1,0:T(8,128)(2,1)} copy(bf16[256,2048]{1,0:T(8,128)(2,1)} %moe.1) | data formatting | bytes 2097152
